TPU v7x, 128 devices: a whole 4x4x4 slice. The times are simulated.
128 devices in a mesh: rows: 16 (over x, z), chan: 8 (over y, core).
Axes of the slice: x: 4, y: 4, z: 4, core: 2. Of those that a mesh axis runs over, the one named last changes fastest.
Arguments:
- frames: bfloat16 [2, 256, 128, 256], P(None, None, 'rows'), may hold values from -6 to 6
- hidden_init: bfloat16 [256, 128, 256], P('chan', 'rows'), may hold values from -3 to 3
- gate_weight: bfloat16 [3, 256, 9, 512], P(None, 'chan'), may hold values from -0.09375 to 0.09375
- readout: bfloat16 [256], P('chan'), may hold values from -1.5 to 1.5
- catchment: int32 [128, 256], P('rows'), may hold values from 0 to 511
- targets: float32 [512], replicated, may hold values from 0.2 to 2
Outputs:
- loss: float32 [], replicated
- gate_grad: float32 [3, 256, 9, 512], P(None, 'chan')
- readout_grad: float32 [256], P('chan')
- hidden_grad: float32 [256, 128, 256], P('chan', 'rows')
All inputs are finite; a program needn't handle non-finite values.
Results may differ from a plain program's by a relative error of at most 0.007.
Values may be sent and summed in bfloat16 or wider, within the bound.
No kernel may reach another device: no remote copies, remote signals or barrier semaphores. Data moves between devices by JAX's collectives and lax.ppermute only.
A program may use at most 128 MiB of HBM per device.

v0:
```python
import jax
import jax.numpy as jnp
from jax import lax
from jax.sharding import PartitionSpec as P


def padded_2(x, sides, width):
    for axis, dim in sides:
        count, length = (lax.axis_size(axis), x.shape[dim])
        up = [(i, (i + 1) % count) for i in range(count - 1)]
        down = [(j, i) for i, j in up]
        last = lax.slice_in_dim(x, length - width, length, axis=dim)
        leading = lax.slice_in_dim(x, 0, width, axis=dim)
        before = lax.ppermute(last, axis, up)
        after = lax.ppermute(leading, axis, down)
        x = jnp.concatenate([before, x, after], axis=dim)
    return x


def pad_columns(field):
    widths = [(0, 0)] * (field.ndim - 1) + [(1, 1)]
    return jnp.pad(field, widths)


def widen(field):
    return lax.all_gather(field, "chan", axis=0, tiled=True)


def with_rims(field):
    return padded_2(field, (("rows", 1),), 1)


def narrow(partial_sum):
    return lax.psum_scatter(partial_sum, "chan", scatter_dimension=0, tiled=True)


def conv_taps(kernel, padded):
    height = padded.shape[1] - 2
    width = padded.shape[2] - 2
    total = None
    for offset in range(9):
        shift_row, shift_col = (offset // 3, offset % 3)
        window = padded[:, shift_row : shift_row + height, shift_col : shift_col + width]
        term = jnp.einsum(
            "goc,crw->gorw", kernel[:, :, offset], window, preferred_element_type=jnp.float32
        )
        total = term if total is None else total + term
    return total


def weight_taps(grad_pre, padded):
    height, width = (grad_pre.shape[2], grad_pre.shape[3])
    pieces = []
    for offset in range(9):
        shift_row, shift_col = (offset // 3, offset % 3)
        window = padded[:, shift_row : shift_row + height, shift_col : shift_col + width]
        pieces.append(
            jnp.einsum("gorw,crw->goc", grad_pre, window, preferred_element_type=jnp.float32)
        )
    return jnp.stack(pieces, axis=2)


def input_taps(kernel, grad_pad):
    height = grad_pad.shape[2] - 2
    width = grad_pad.shape[3] - 2
    total = None
    for offset in range(9):
        shift_row, shift_col = (offset // 3, offset % 3)
        window = grad_pad[
            :, :, 2 - shift_row : 2 - shift_row + height, 2 - shift_col : 2 - shift_col + width
        ]
        term = jnp.einsum(
            "goc,gorw->crw", kernel[:, :, offset], window, preferred_element_type=jnp.float32
        )
        total = term if total is None else total + term
    return total


def grad_rims(grad_pre):
    gates, outputs, height, width = grad_pre.shape
    flat = grad_pre.reshape(gates * outputs, height, width)
    return pad_columns(with_rims(flat)).reshape(gates, outputs, height + 2, width + 2)


def forward_step(frame, state, w_frame, w_state):
    frame_depth = frame.shape[0]
    whole = widen(state)
    padded = pad_columns(with_rims(jnp.concatenate([frame, whole], axis=0)))
    frame_pad = padded[:frame_depth]
    state_pad = padded[frame_depth:]
    from_frame = conv_taps(w_frame, frame_pad)
    both = from_frame[0:2] + conv_taps(w_state[0:2], state_pad)
    update = jax.nn.sigmoid(both[0])
    reset = jax.nn.sigmoid(both[1])
    state_f = state.astype(jnp.float32)
    reset_state = (reset * state_f).astype(jnp.bfloat16)
    reset_pad = pad_columns(with_rims(widen(reset_state)))
    candidate = jnp.tanh(from_frame[2] + conv_taps(w_state[2:3], reset_pad)[0])
    new_state = ((1.0 - update) * state_f + update * candidate).astype(jnp.bfloat16)
    return (new_state, (frame_pad, state_pad, reset_pad, state_f, update, reset, candidate))


def backward_step(grad_state, kept, w_state):
    frame_pad, state_pad, reset_pad, state_f, update, reset, candidate = kept
    grad_update = grad_state * (candidate - state_f)
    grad_cand = grad_state * update
    carry = grad_state * (1.0 - update)
    pre_cand = (grad_cand * (1.0 - candidate * candidate)).astype(jnp.bfloat16)[None]
    cand_grad = jnp.concatenate(
        [weight_taps(pre_cand, frame_pad), weight_taps(pre_cand, reset_pad)], axis=-1
    )
    grad_reset_state = narrow(input_taps(w_state[2:3], grad_rims(pre_cand)))
    grad_reset = grad_reset_state * state_f
    carry = carry + grad_reset_state * reset
    pre_both = jnp.stack(
        [grad_update * update * (1.0 - update), grad_reset * reset * (1.0 - reset)]
    ).astype(jnp.bfloat16)
    both_grad = jnp.concatenate(
        [weight_taps(pre_both, frame_pad), weight_taps(pre_both, state_pad)], axis=-1
    )
    grad_prev = carry + narrow(input_taps(w_state[0:2], grad_rims(pre_both)))
    return (grad_prev, jnp.concatenate([both_grad, cand_grad], axis=0))


def per_device(frames, hidden_init, gate_weight, readout, catchment, targets):
    frame_depth = frames.shape[1]
    w_frame = gate_weight[..., :frame_depth]
    w_state = gate_weight[..., frame_depth:]
    state = hidden_init
    states = []
    saved = []
    for step in range(frames.shape[0]):
        states.append(state)
        state, kept = forward_step(frames[step], state, w_frame, w_state)
        saved.append(kept)
    rain = jnp.einsum("c,crw->rw", readout, state, preferred_element_type=jnp.float32)
    catchments = targets.shape[0]
    labels = catchment.reshape(-1)
    onehot = (labels[:, None] == jnp.arange(catchments, dtype=jnp.int32)[None, :]).astype(
        jnp.float32
    )
    local_totals = jnp.dot(rain.reshape(-1), onehot, precision=lax.Precision.HIGHEST)
    leader = (lax.axis_index("chan") == 0).astype(jnp.float32)
    local_counts = jnp.sum(onehot, axis=0) * leader
    totals, counts = lax.psum((local_totals, local_counts), ("rows", "chan"))
    scale = 1.0 / (counts + 1.0)
    mean_rate = totals * scale
    rate = jax.nn.softplus(mean_rate)
    miss = rate - targets
    loss = 0.5 * jnp.mean(miss * miss)
    grad_mean = miss / catchments * jax.nn.sigmoid(mean_rate) * scale
    grad_rain = jnp.dot(onehot, grad_mean, precision=lax.Precision.HIGHEST).reshape(rain.shape)
    state_f = state.astype(jnp.float32)
    readout_part = jnp.einsum("crw,rw->c", state_f, grad_rain)
    grad_state = readout.astype(jnp.float32)[:, None, None] * grad_rain[None]
    gate_part = jnp.zeros(gate_weight.shape, jnp.float32)
    for step in reversed(range(frames.shape[0])):
        kept = saved[step]
        grad_state, step_grad = backward_step(grad_state, kept, w_state)
        gate_part = gate_part + step_grad
    gate_grad, readout_grad = lax.psum((gate_part, readout_part), "rows")
    return (loss, gate_grad, readout_grad, grad_state)


def solution(mesh):
    in_specs = (
        P(None, None, "rows", None),
        P("chan", "rows", None),
        P(None, "chan", None, None),
        P("chan"),
        P("rows", None),
        P(),
    )
    out_specs = (P(), P(None, "chan", None, None), P("chan"), P("chan", "rows", None))
    return jax.shard_map(
        per_device, mesh=mesh, in_specs=in_specs, out_specs=out_specs, check_vma=False
    )
```

profile of v0, /device:TPU:0, one launch (start us, length us, event | category | flops | bytes accessed | tf_op | source)
XLA Modules:
  0.0 618.4 jit_solution(15660473705716595447)
XLA Ops:
  7.2 1.6 copy.190
  8.9 2.6 fusion.599
  12.5 23.6 %all-gather.5.cloned.1.call-done = bf16[256,8,256]{2,0,1:T(8,128)(2,1)} async-done(((bf16[32,8,256]{2,0,1:T(8,128)(2,1)}), bf16[256,8,256]{2,0,1:T(8,128)(2,1)}) %all-gather.5.cloned.1.call-update) | async-done | bytes 1048592 | tf_op jit(solution)/shard_map/all_gather | solution.py:26
  37.2 3.5 collective-permute-start
  40.7 1.4 collective-permute-start.1
  42.2 4.5 collective-permute-done
  46.7 4.3 collective-permute-done.1
  51.0 4.8 fusion.10
  65.9 24.5 %all-gather.7.cloned.1.call-done = bf16[256,8,256]{2,0,1:T(8,128)(2,1)} async-done(((bf16[32,8,256]{2,0,1:T(8,128)(2,1)}), bf16[256,8,256]{2,0,1:T(8,128)(2,1)}) %all-gather.7.cloned.1.call-update) | async-done | bytes 1048592 | tf_op jit(solution)/shard_map/all_gather | solution.py:26
  91.5 3.5 collective-permute-start.2
  95.0 1.5 collective-permute-start.3
  96.5 1.5 fusion.522
  98.1 4.1 collective-permute-done.3
  111.0 2.2 fusion.294
  113.3 2.4 copy.460
  115.7 22.1 %all-gather.9.cloned.1.call-done = bf16[256,8,256]{2,0,1:T(8,128)(2,1)} async-done(((bf16[32,8,256]{2,0,1:T(8,128)(2,1)}), bf16[256,8,256]{2,0,1:T(8,128)(2,1)}) %all-gather.9.cloned.1.call-update) | async-done | bytes 1048592 | tf_op jit(solution)/shard_map/all_gather | solution.py:26
  139.1 3.5 collective-permute-start.4
  142.6 1.3 collective-permute-start.5
  144.2 4.3 collective-permute-done.4
  148.5 4.1 collective-permute-done.5
  152.7 4.8 select_maximum_fusion
  168.2 23.3 %all-gather.11.cloned.1.call-done = bf16[256,8,256]{2,0,1:T(8,128)(2,1)} async-done(((bf16[32,8,256]{2,0,1:T(8,128)(2,1)}), bf16[256,8,256]{2,0,1:T(8,128)(2,1)}) %all-gather.11.cloned.1.call-update) | async-done | bytes 1048592 | tf_op jit(solution)/shard_map/all_gather | solution.py:26
  192.6 3.5 collective-permute-start.6
  196.1 1.5 collective-permute-start.7
  197.6 1.5 fusion.524
  199.2 4.1 collective-permute-done.7
  212.1 2.2 fusion.304
  215.1 2.0 fusion.2
  217.1 65.9 %all-reduce.8 = (f32[512]{0:T(512)}, f32[512]{0:T(512)}) all-reduce(f32[512]{0:T(512)} %bitcast.1400, f32[512]{0:T(512)S(1)} %broadcast_multiply_fusion), channel_id=1, replica_groups=mesh['rows'=16,'chan'=8] {'rows','chan'}, use_global_device_ids=true, to_apply=%region_0.1 | all-reduce | flops 1024 | bytes 8192 | tf_op jit(solution)/shard_map/psum | solution.py:145
  283.0 1.3 fusion.578
  284.3 2.8 fusion.1
  289.0 2.0 collective-permute-start.8
  291.0 1.3 collective-permute-start.9
  293.6 3.1 collective-permute-done.9
  306.5 3.3 add_bitcast_fusion.1
  310.3 1.8 fusion.113
  312.1 1.7 fusion.112
  326.3 18.7 %reduce-scatter.5.cloned.1.call-done = f32[32,8,256]{2,0,1:T(8,128)} async-done(((f32[256,8,256]{2,0,1:T(8,128)}), f32[32,8,256]{2,0,1:T(8,128)}) %reduce-scatter.5.cloned.1.call-update) | async-done | bytes 262160 | tf_op jit(solution)/shard_map/reduce_scatter | solution.py:34
  345.0 1.4 fusion.311
  346.7 3.4 collective-permute-start.10
  350.1 1.3 collective-permute-start.11
  351.4 2.5 fusion.114
  354.0 2.3 collective-permute-done.11
  367.1 3.4 fusion.15
  371.5 2.4 fusion.77
  373.9 2.2 fusion.76
  393.8 10.6 %reduce-scatter.7.cloned.1.call-done = f32[32,8,256]{2,0,1:T(8,128)} async-done(((f32[256,8,256]{2,0,1:T(8,128)}), f32[32,8,256]{2,0,1:T(8,128)}) %reduce-scatter.7.cloned.1.call-update) | async-done | bytes 262160 | tf_op jit(solution)/shard_map/reduce_scatter | solution.py:34
  404.4 2.2 fusion.299
  406.8 3.4 collective-permute-start.12
  410.1 1.3 collective-permute-start.13
  411.9 3.9 collective-permute-done.13
  425.7 3.3 add_bitcast_fusion
  429.3 1.7 fusion.94
  444.6 18.5 %reduce-scatter.9.cloned.1.call-done = f32[32,8,256]{2,0,1:T(8,128)} async-done(((f32[256,8,256]{2,0,1:T(8,128)}), f32[32,8,256]{2,0,1:T(8,128)}) %reduce-scatter.9.cloned.1.call-update) | async-done | bytes 262160 | tf_op jit(solution)/shard_map/reduce_scatter | solution.py:34
  464.2 1.8 fusion.68
  466.0 1.7 fusion.59
  468.0 3.4 collective-permute-start.14
  471.4 1.4 collective-permute-start.15
  480.7 2.9 maximum_add_fusion
  494.8 3.4 fusion.14
  499.2 42.0 %psum.31 = f32[32]{0:T(128)} all-reduce(f32[32]{0:T(128)S(1)} %convolution_bitcast_fusion.84), channel_id=1, replica_groups=mesh['rows'=16,'chan'=8] {'rows'}, use_global_device_ids=true, to_apply=%region_8.9 | all-reduce | flops 32 | bytes 256 | tf_op jit(solution)/shard_map/psum | solution.py:161
  541.3 31.8 %all-reduce.11.cloned.1.call-done = f32[3,32,9,512]{3,1,0,2:T(8,128)} async-done(((f32[3,32,9,512]{3,1,0,2:T(8,128)}), f32[3,32,9,512]{3,1,0,2:T(8,128)}) %all-reduce.11.cloned.1.call-update) | async-done | bytes 1769488 | tf_op jit(solution)/shard_map/psum | solution.py:161
  573.1 2.9 copy.269
  576.0 32.3 %reduce-scatter.11.cloned.1.call-done = f32[32,8,256]{2,0,1:T(8,128)} async-done(((f32[256,8,256]{2,0,1:T(8,128)}), f32[32,8,256]{2,0,1:T(8,128)}) %reduce-scatter.11.cloned.1.call-update) | async-done | bytes 262160 | tf_op jit(solution)/shard_map/reduce_scatter | solution.py:34
  (397 shorter events, 146.7 us)
Async XLA Ops:
  7.2 29.0 %all-gather.5.cloned.1.call-start = ((), (), s32[]{:S(2)}) async-start(), calls=%async_computation.4 | async-start | bytes 1179648 | tf_op jit(solution)/shard_map/all_gather | solution.py:26
  8.8 81.6 %all-gather.7.cloned.1.call-start = ((), (), s32[]{:S(2)}) async-start(), calls=%async_computation.5 | async-start | bytes 1179648 | tf_op jit(solution)/shard_map/all_gather | solution.py:26
  12.5 51.2 %copy-start.9 = (bf16[1,256,8,256]{3,1,2,0:T(8,128)(2,1)}, bf16[1,256,8,256]{3,1,2,0:T(8,128)(2,1)S(1)}, u32[]{:S(2)}) copy-start(bf16[1,256,8,256]{3,1,2,0:T(8,128)(2,1)S(1)} %copy.459) | copy-start | bytes 3145732
  36.1 14.8 %copy-start.8 = (bf16[256,8,256]{2,0,1:T(8,128)(2,1)S(1)}, bf16[256,8,256]{2,0,1:T(8,128)(2,1)}, u32[]{:S(2)}) copy-start(bf16[256,8,256]{2,0,1:T(8,128)(2,1)} %all-gather.5.cloned.1.call-done) | copy-start | bytes 3145732
  37.2 9.4 %collective-permute-start = (bf16[512,1,256]{2,0,1:T(8,128)(2,1)S(1)}, bf16[512,1,256]{2,0,1:T(8,128)(2,1)S(1)}, u32[]{:S(2)}, u32[]{:S(2)}) collective-permute-start(bf16[512,1,256]{2,0,1:T(8,128)(2,1)S(1)} %get-tuple-element.28), channel_id=1, source_target_pairs={{0,8},{8,16},{16,24},{24,32},{32,40},{40,48},{48,56},{56,64},{64,7... | collective-permute-start | bytes 786440 | tf_op jit(solution)/shard_map/ppermute | solution.py:14
  40.7 15.1 %copy-start.44 = (bf16[3,32,9,512]{3,1,2,0:T(8,128)(2,1)S(1)}, bf16[3,32,9,512]{3,1,2,0:T(8,128)(2,1)}, u32[]{:S(2)}) copy-start(bf16[3,32,9,512]{3,1,2,0:T(8,128)(2,1)} %param.8) | copy-start | bytes 2654212
  40.7 10.2 %collective-permute-start.1 = (bf16[512,1,256]{2,0,1:T(8,128)(2,1)S(1)}, bf16[512,1,256]{2,0,1:T(8,128)(2,1)S(1)}, u32[]{:S(2)}, u32[]{:S(2)}) collective-permute-start(bf16[512,1,256]{2,0,1:T(8,128)(2,1)S(1)} %get-tuple-element.29), channel_id=1, source_target_pairs={{8,0},{16,8},{24,16},{32,24},{40,32},{48,40},{56,48},{64,56},{72,6... | collective-permute-start | bytes 786440 | tf_op jit(solution)/shard_map/ppermute | solution.py:15
  46.7 12.6 %copy-start.66 = (bf16[512,1,256]{2,0,1:T(8,128)(2,1)}, bf16[512,1,256]{2,0,1:T(8,128)(2,1)S(1)}, u32[]{:S(2)}) copy-start(bf16[512,1,256]{2,0,1:T(8,128)(2,1)S(1)} %collective-permute-done) | copy-start | bytes 786436
  51.0 12.7 %copy-start.64 = (bf16[512,1,256]{2,0,1:T(8,128)(2,1)}, bf16[512,1,256]{2,0,1:T(8,128)(2,1)S(1)}, u32[]{:S(2)}) copy-start(bf16[512,1,256]{2,0,1:T(8,128)(2,1)S(1)} %collective-permute-done.1) | copy-start | bytes 786436
  55.8 8.2 %copy-start = (bf16[512,10,258]{2,0,1:T(8,128)(2,1)}, bf16[512,10,258]{2,0,1:T(8,128)(2,1)S(1)}, u32[]{:S(2)}) copy-start(bf16[512,10,258]{2,0,1:T(8,128)(2,1)S(1)} %fusion.10) | copy-start | bytes 7925764
  64.9 46.0 %copy-start.40 = (f32[2,32,8,256]{3,1,2,0:T(8,128)}, f32[2,32,8,256]{3,1,2,0:T(8,128)S(1)}, u32[]{:S(2)}) copy-start(f32[2,32,8,256]{3,1,2,0:T(8,128)S(1)} %fusion.30) | copy-start | bytes 1572868
  65.8 72.0 %all-gather.9.cloned.1.call-start = ((), (), s32[]{:S(2)}) async-start(), calls=%async_computation.6 | async-start | bytes 1179648 | tf_op jit(solution)/shard_map/all_gather | solution.py:26
  90.4 11.8 %copy-start.36 = (bf16[256,8,256]{2,0,1:T(8,128)(2,1)S(1)}, bf16[256,8,256]{2,0,1:T(8,128)(2,1)}, u32[]{:S(2)}) copy-start(bf16[256,8,256]{2,0,1:T(8,128)(2,1)} %all-gather.7.cloned.1.call-done) | copy-start | bytes 3145732
  91.5 6.6 %collective-permute-start.2 = (bf16[256,1,256]{2,0,1:T(8,128)(2,1)S(1)}, bf16[256,1,256]{2,0,1:T(8,128)(2,1)S(1)}, u32[]{:S(2)}, u32[]{:S(2)}) collective-permute-start(bf16[256,1,256]{2,0,1:T(8,128)(2,1)S(1)} %get-tuple-element.32), channel_id=1, source_target_pairs={{0,8},{8,16},{16,24},{24,32},{32,40},{40,48},{48,56},{56,64},{64,7... | collective-permute-start | bytes 393224 | tf_op jit(solution)/shard_map/ppermute | solution.py:14
  95.0 7.3 %collective-permute-start.3 = (bf16[256,1,256]{2,0,1:T(8,128)(2,1)S(1)}, bf16[256,1,256]{2,0,1:T(8,128)(2,1)S(1)}, u32[]{:S(2)}, u32[]{:S(2)}) collective-permute-start(bf16[256,1,256]{2,0,1:T(8,128)(2,1)S(1)} %get-tuple-element.33), channel_id=1, source_target_pairs={{8,0},{16,8},{24,16},{32,24},{40,32},{48,40},{56,48},{64,56},{72,6... | collective-permute-start | bytes 393224 | tf_op jit(solution)/shard_map/ppermute | solution.py:15
  98.1 9.7 %copy-start.81 = (bf16[256,1,256]{2,0,1:T(8,128)(2,1)}, bf16[256,1,256]{2,0,1:T(8,128)(2,1)S(1)}, u32[]{:S(2)}) copy-start(bf16[256,1,256]{2,0,1:T(8,128)(2,1)S(1)} %collective-permute-done.2) | copy-start | bytes 393220
  102.3 7.7 %copy-start.79 = (bf16[256,1,256]{2,0,1:T(8,128)(2,1)}, bf16[256,1,256]{2,0,1:T(8,128)(2,1)S(1)}, u32[]{:S(2)}) copy-start(bf16[256,1,256]{2,0,1:T(8,128)(2,1)S(1)} %collective-permute-done.3) | copy-start | bytes 393220
  113.2 78.3 %all-gather.11.cloned.1.call-start = ((), (), s32[]{:S(2)}) async-start(), calls=%async_computation.7 | async-start | bytes 1179648 | tf_op jit(solution)/shard_map/all_gather | solution.py:26
  137.8 6.1 copy-start.11
  137.8 6.1 copy-start.45
  137.8 14.9 %copy-start.19 = (bf16[1,256,8,256]{3,1,2,0:T(8,128)(2,1)S(1)}, bf16[1,256,8,256]{3,1,2,0:T(8,128)(2,1)}, u32[]{:S(2)}) copy-start(bf16[1,256,8,256]{3,1,2,0:T(8,128)(2,1)} %copy.460) | copy-start | bytes 3145732
  139.1 9.4 %collective-permute-start.4 = (bf16[512,1,256]{2,0,1:T(8,128)(2,1)S(1)}, bf16[512,1,256]{2,0,1:T(8,128)(2,1)S(1)}, u32[]{:S(2)}, u32[]{:S(2)}) collective-permute-start(bf16[512,1,256]{2,0,1:T(8,128)(2,1)S(1)} %get-tuple-element.22), channel_id=1, source_target_pairs={{0,8},{8,16},{16,24},{24,32},{32,40},{40,48},{48,56},{56,64},{64,7... | collective-permute-start | bytes 786440 | tf_op jit(solution)/shard_map/ppermute | solution.py:14
  142.6 10.1 %collective-permute-start.5 = (bf16[512,1,256]{2,0,1:T(8,128)(2,1)S(1)}, bf16[512,1,256]{2,0,1:T(8,128)(2,1)S(1)}, u32[]{:S(2)}, u32[]{:S(2)}) collective-permute-start(bf16[512,1,256]{2,0,1:T(8,128)(2,1)S(1)} %get-tuple-element.23), channel_id=1, source_target_pairs={{8,0},{16,8},{24,16},{32,24},{40,32},{48,40},{56,48},{64,56},{72,6... | collective-permute-start | bytes 786440 | tf_op jit(solution)/shard_map/ppermute | solution.py:15
  148.5 14.9 %copy-start.70 = (bf16[512,1,256]{2,0,1:T(8,128)(2,1)}, bf16[512,1,256]{2,0,1:T(8,128)(2,1)S(1)}, u32[]{:S(2)}) copy-start(bf16[512,1,256]{2,0,1:T(8,128)(2,1)S(1)} %collective-permute-done.4) | copy-start | bytes 786436
  152.7 12.1 %copy-start.68 = (bf16[512,1,256]{2,0,1:T(8,128)(2,1)}, bf16[512,1,256]{2,0,1:T(8,128)(2,1)S(1)}, u32[]{:S(2)}) copy-start(bf16[512,1,256]{2,0,1:T(8,128)(2,1)S(1)} %collective-permute-done.5) | copy-start | bytes 786436
  157.5 7.7 %copy-start.5 = (bf16[512,10,258]{2,0,1:T(8,128)(2,1)}, bf16[512,10,258]{2,0,1:T(8,128)(2,1)S(1)}, u32[]{:S(2)}) copy-start(bf16[512,10,258]{2,0,1:T(8,128)(2,1)S(1)} %select_maximum_fusion) | copy-start | bytes 7925764
  166.1 121.7 %copy-start.34 = (f32[2,32,8,256]{3,1,2,0:T(8,128)}, f32[2,32,8,256]{3,1,2,0:T(8,128)S(1)}, u32[]{:S(2)}) copy-start(f32[2,32,8,256]{3,1,2,0:T(8,128)S(1)} %slice_add_fusion) | copy-start | bytes 1572868
  166.9 178.1 %reduce-scatter.5.cloned.1.call-start = ((), (), s32[]{:S(2)}) async-start(), calls=%async_computation.8 | async-start | bytes 2359296 | tf_op jit(solution)/shard_map/reduce_scatter | solution.py:34
  191.5 11.8 %copy-start.38 = (bf16[256,8,256]{2,0,1:T(8,128)(2,1)S(1)}, bf16[256,8,256]{2,0,1:T(8,128)(2,1)}, u32[]{:S(2)}) copy-start(bf16[256,8,256]{2,0,1:T(8,128)(2,1)} %all-gather.11.cloned.1.call-done) | copy-start | bytes 3145732
  192.6 6.6 %collective-permute-start.6 = (bf16[256,1,256]{2,0,1:T(8,128)(2,1)S(1)}, bf16[256,1,256]{2,0,1:T(8,128)(2,1)S(1)}, u32[]{:S(2)}, u32[]{:S(2)}) collective-permute-start(bf16[256,1,256]{2,0,1:T(8,128)(2,1)S(1)} %get-tuple-element.30), channel_id=1, source_target_pairs={{0,8},{8,16},{16,24},{24,32},{32,40},{40,48},{48,56},{56,64},{64,7... | collective-permute-start | bytes 393224 | tf_op jit(solution)/shard_map/ppermute | solution.py:14
  196.1 7.3 %collective-permute-start.7 = (bf16[256,1,256]{2,0,1:T(8,128)(2,1)S(1)}, bf16[256,1,256]{2,0,1:T(8,128)(2,1)S(1)}, u32[]{:S(2)}, u32[]{:S(2)}) collective-permute-start(bf16[256,1,256]{2,0,1:T(8,128)(2,1)S(1)} %get-tuple-element.31), channel_id=1, source_target_pairs={{8,0},{16,8},{24,16},{32,24},{40,32},{48,40},{56,48},{64,56},{72,6... | collective-permute-start | bytes 393224 | tf_op jit(solution)/shard_map/ppermute | solution.py:15
  199.2 9.8 %copy-start.84 = (bf16[256,1,256]{2,0,1:T(8,128)(2,1)}, bf16[256,1,256]{2,0,1:T(8,128)(2,1)S(1)}, u32[]{:S(2)}) copy-start(bf16[256,1,256]{2,0,1:T(8,128)(2,1)S(1)} %collective-permute-done.6) | copy-start | bytes 393220
  203.3 7.7 %copy-start.82 = (bf16[256,1,256]{2,0,1:T(8,128)(2,1)}, bf16[256,1,256]{2,0,1:T(8,128)(2,1)S(1)}, u32[]{:S(2)}) copy-start(bf16[256,1,256]{2,0,1:T(8,128)(2,1)S(1)} %collective-permute-done.7) | copy-start | bytes 393220
  204.5 7.6 %copy-start.3 = (bf16[256,10,258]{2,0,1:T(8,128)(2,1)}, bf16[256,10,258]{2,0,1:T(8,128)(2,1)S(1)}, u32[]{:S(2)}) copy-start(bf16[256,10,258]{2,0,1:T(8,128)(2,1)S(1)} %select_maximum_fusion.2) | copy-start | bytes 3962884
  211.1 3.9 copy-start.91
  211.1 4.0 copy-start.89
  289.0 4.6 collective-permute-start.8
  291.0 5.6 collective-permute-start.9
  309.9 94.5 %reduce-scatter.7.cloned.1.call-start = ((), (), s32[]{:S(2)}) async-start(), calls=%async_computation.9 | async-start | bytes 2359296 | tf_op jit(solution)/shard_map/reduce_scatter | solution.py:34
  318.9 4.2 copy-start.77
  323.1 21.9 %copy-start.46 = (f32[8,256,32]{1,2,0:T(8,128)S(1)}, f32[8,256,32]{1,2,0:T(8,128)}, u32[]{:S(2)}) copy-start(f32[8,256,32]{1,2,0:T(8,128)} %get-tuple-element.49) | copy-start | bytes 786436
  323.1 21.9 %copy-start.52 = (bf16[32,8,256]{2,0,1:T(8,128)(2,1)S(1)}, bf16[32,8,256]{2,0,1:T(8,128)(2,1)}, u32[]{:S(2)}) copy-start(bf16[32,8,256]{2,0,1:T(8,128)(2,1)} %get-tuple-element.46) | copy-start | bytes 393220
  346.4 10.3 %copy-start.54 = (bf16[1,32,8,256]{3,1,2,0:T(8,128)(2,1)}, bf16[1,32,8,256]{3,1,2,0:T(8,128)(2,1)S(1)}, u32[]{:S(2)}) copy-start(bf16[1,32,8,256]{3,1,2,0:T(8,128)(2,1)S(1)} %get-tuple-element.34) | copy-start | bytes 393220
  346.4 10.3 %copy-start.57 = (bf16[1,32,8,256]{3,1,2,0:T(8,128)(2,1)}, bf16[1,32,8,256]{3,1,2,0:T(8,128)(2,1)S(1)}, u32[]{:S(2)}) copy-start(bf16[1,32,8,256]{3,1,2,0:T(8,128)(2,1)S(1)} %get-tuple-element.35) | copy-start | bytes 393220
  346.7 7.2 %collective-permute-start.10 = (bf16[64,1,256]{2,1,0:T(2,128)(2,1)S(1)}, bf16[64,1,256]{2,1,0:T(2,128)(2,1)S(1)}, u32[]{:S(2)}, u32[]{:S(2)}) collective-permute-start(bf16[64,1,256]{2,1,0:T(2,128)(2,1)S(1)} %get-tuple-element.38), channel_id=1, source_target_pairs={{0,8},{8,16},{16,24},{24,32},{32,40},{40,48},{48,56},{56,64},{64,7... | collective-permute-start | bytes 98312 | tf_op jit(solution)/shard_map/ppermute | solution.py:14
  350.1 6.2 collective-permute-start.11
  370.6 92.5 %reduce-scatter.9.cloned.1.call-start = ((), (), s32[]{:S(2)}) async-start(), calls=%async_computation.10 | async-start | bytes 2359296 | tf_op jit(solution)/shard_map/reduce_scatter | solution.py:34
  371.5 4.7 copy-start.7
  390.4 14.0 %copy-start.35 = (f32[2,32,8,256]{3,1,2,0:T(8,128)S(1)}, f32[2,32,8,256]{3,1,2,0:T(8,128)}, u32[]{:S(2)}) copy-start(f32[2,32,8,256]{3,1,2,0:T(8,128)} %copy-done.34) | copy-start | bytes 1572868
  406.7 10.5 %copy-start.62 = (f32[32,8,256]{2,0,1:T(8,128)}, f32[32,8,256]{2,0,1:T(8,128)S(1)}, u32[]{:S(2)}) copy-start(f32[32,8,256]{2,0,1:T(8,128)S(1)} %get-tuple-element.19) | copy-start | bytes 786436
  406.8 5.1 collective-permute-start.12
  410.1 5.6 collective-permute-start.13
  429.0 144.1 %all-reduce.11.cloned.1.call-start = ((), (), s32[]{:S(2)}) async-start(), calls=%async_computation.11 | async-start | bytes 3538944 | tf_op jit(solution)/shard_map/psum | solution.py:161
  436.0 4.2 copy-start.75
  441.4 21.7 %copy-start.42 = (f32[2,32,8,256]{3,1,2,0:T(8,128)S(1)}, f32[2,32,8,256]{3,1,2,0:T(8,128)}, u32[]{:S(2)}) copy-start(f32[2,32,8,256]{3,1,2,0:T(8,128)} %copy-done.40) | copy-start | bytes 1572868
  441.4 21.7 %copy-start.49 = (bf16[32,8,256]{2,1,0:T(8,128)(2,1)S(1)}, bf16[32,8,256]{2,1,0:T(8,128)(2,1)}, u32[]{:S(2)}) copy-start(bf16[32,8,256]{2,1,0:T(8,128)(2,1)} %param.7) | copy-start | bytes 393220
  441.4 22.8 %copy-start.53 = (bf16[1,32,8,256]{3,1,2,0:T(8,128)(2,1)S(1)}, bf16[1,32,8,256]{3,1,2,0:T(8,128)(2,1)}, u32[]{:S(2)}) copy-start(bf16[1,32,8,256]{3,1,2,0:T(8,128)(2,1)} %get-tuple-element.18) | copy-start | bytes 393220
  464.2 8.7 %copy-start.18 = (bf16[256,8,256]{2,0,1:T(8,128)(2,1)S(1)}, bf16[256,8,256]{2,0,1:T(8,128)(2,1)}, u32[]{:S(2)}) copy-start(bf16[256,8,256]{2,0,1:T(8,128)(2,1)} %copy-done.16) | copy-start | bytes 3145732
  464.2 9.1 %copy-start.2 = (bf16[512,10,258]{2,0,1:T(8,128)(2,1)S(1)}, bf16[512,10,258]{2,0,1:T(8,128)(2,1)}, u32[]{:S(2)}) copy-start(bf16[512,10,258]{2,0,1:T(8,128)(2,1)} %copy-done) | copy-start | bytes 7925764
  468.0 16.0 %collective-permute-start.14 = (bf16[64,1,256]{2,1,0:T(2,128)(2,1)S(1)}, bf16[64,1,256]{2,1,0:T(2,128)(2,1)S(1)}, u32[]{:S(2)}, u32[]{:S(2)}) collective-permute-start(bf16[64,1,256]{2,1,0:T(2,128)(2,1)S(1)} %get-tuple-element.36), channel_id=1, source_target_pairs={{0,8},{8,16},{16,24},{24,32},{32,40},{40,48},{48,56},{56,64},{64,7... | collective-permute-start | bytes 98312 | tf_op jit(solution)/shard_map/ppermute | solution.py:14
  471.4 12.6 %collective-permute-start.15 = (bf16[64,1,256]{2,1,0:T(2,128)(2,1)S(1)}, bf16[64,1,256]{2,1,0:T(2,128)(2,1)S(1)}, u32[]{:S(2)}, u32[]{:S(2)}) collective-permute-start(bf16[64,1,256]{2,1,0:T(2,128)(2,1)S(1)} %get-tuple-element.37), channel_id=1, source_target_pairs={{8,0},{16,8},{24,16},{32,24},{40,32},{48,40},{56,48},{64,56},{72,6... | collective-permute-start | bytes 98312 | tf_op jit(solution)/shard_map/ppermute | solution.py:15
  483.7 124.7 %reduce-scatter.11.cloned.1.call-start = ((), (), s32[]{:S(2)}) async-start(), calls=%async_computation.12 | async-start | bytes 2359296 | tf_op jit(solution)/shard_map/reduce_scatter | solution.py:34
  498.2 110.1 %copy-start.63 = (f32[32,8,256]{2,0,1:T(8,128)S(1)}, f32[32,8,256]{2,0,1:T(8,128)}, u32[]{:S(2)}) copy-start(f32[32,8,256]{2,0,1:T(8,128)} %copy-done.62) | copy-start | bytes 786436
  498.2 110.1 %copy-start.72 = (f32[32,8,256]{2,0,1:T(8,128)S(1)}, f32[32,8,256]{2,0,1:T(8,128)}, u32[]{:S(2)}) copy-start(f32[32,8,256]{2,0,1:T(8,128)} %reduce-scatter.9.cloned.1.call-done) | copy-start | bytes 786436
  (53 other events, 103.7 us)
Sparse Core Ops, SparseCore 0:
  10.3 25.8 all-gather.4
  66.0 24.4 all-gather.6
  113.3 24.4 all-gather.8
  167.0 24.4 all-gather.10
  310.0 34.9 reduce-scatter.4
  370.7 33.6 reduce-scatter.6
  429.1 33.9 reduce-scatter.8
  483.8 89.2 all-reduce.10
  575.5 32.7 reduce-scatter.10
where the time goes:
time: 630 us; the launch traced here: 618 us
  waiting for transfers between devices  241 us (38%)
  matrix products  160 us (25%)
  blocking collectives  108 us (17%)
  starting transfers between devices  38.5 us (6%)
  other arithmetic  30.6 us (5%)
  local copies, waits for them, and re-layouts  22.4 us (4%)
  between operations  17.8 us (3%)
    all_gather x4, waiting for transfers between devices, widen(): return lax.all_gather(field, 'chan', axis=0, tiled=True)  93.6 us
    reduce_scatter x4, waiting for transfers between devices, narrow(): lax.psum_scatter(partial_sum, 'chan', scatter_dimension=0, tiled=True)  80.1 us
    psum x1, blocking collectives, per_device(): totals, counts = lax.psum((local_totals, local_counts), ('rows', 'chan'))  65.9 us
    dot_general x72, matrix products, weight_taps(): jnp.einsum('gorw,crw->goc', grad_pre, window, preferred_element_type=jnp....  65.5 us
    dot_general x36, matrix products, input_taps(): jnp.einsum('goc,gorw->crw', kernel[:, :, offset], window, preferred_eleme...  53 us
    psum x1, blocking collectives, per_device(): gate_grad, readout_grad = lax.psum((gate_part, readout_part), 'rows')  42 us
    dot_general x54, matrix products, conv_taps(): jnp.einsum('goc,crw->gorw', kernel[:, :, offset], window, preferred_eleme...  36.9 us
    psum x1, waiting for transfers between devices, per_device(): gate_grad, readout_grad = lax.psum((gate_part, readout_part), 'rows')  31.8 us
  transfers between devices with their start and end apart: 25, of which 20 were waited for; matrix products, arithmetic and copies ran while one was open for 15% of the time, Pallas kernels for 0%

commit v1 on v0

v1 whole, which is shorter than its diff:
```python
import functools

import jax
import jax.numpy as jnp
from jax import lax
from jax.experimental import pallas as pl
from jax.experimental.pallas import tpu as pltpu
from jax.sharding import PartitionSpec as P

BF = jnp.bfloat16
F32 = jnp.float32
PITCH = 48
RIM = 8
ROWS_IN = 24
PIX = ROWS_IN * PITCH
OWN_COLS = 32
OWN = 8 * OWN_COLS
C = 256
K = 512
SLOTS = 28
VMEM_LIMIT = 56 * 1024 * 1024


def sigmoid(x):
    return 0.5 * jnp.tanh(0.5 * x) + 0.5


def put(dst, row, count, lane, stride, left_first, x):
    before = pltpu.roll(x, 1, axis=0)
    after = pltpu.roll(x, count - 1, axis=0)
    order = (before, x, after) if left_first else (after, x, before)
    for b in range(3):
        dst[row : row + count, b * stride + lane : b * stride + lane + C] = order[b].astype(BF)


def own_pixels(x):
    return x.reshape(8, PITCH, C)[:, RIM : RIM + OWN_COLS].reshape(OWN, C)


def wide(lab):
    return jnp.concatenate([lab, lab], axis=1)


def conv(xc, w, gate, start, count):
    total = None
    for a in range(3):
        lhs = xc[pl.ds(start + (a - 1) * PITCH, count), :]
        rhs = jnp.concatenate([w[:, gate, 3 * a + b].reshape(C, 2 * C) for b in range(3)], axis=1)
        term = lax.dot_general(lhs, rhs, (((1,), (1,)), ((), ())), preferred_element_type=F32)
        total = term if total is None else total + term
    return total


def forward_kernel(
    x, w, lab, ro, u1, q1, c1, s1, u0, q0, c0, s2, v, tot, xc, ub, qb, sb
):
    def halo_block(field):
        return field.reshape(10, PITCH, C)[:, RIM : RIM + OWN_COLS].reshape(10 * OWN_COLS, C).astype(BF)

    sb[...] = x[2].astype(F32)
    for step in range(2):
        first = 1 + 2 * step
        count = (ROWS_IN - 2 * first) * PITCH
        start = first * PITCH
        put(xc, 0, PIX, 0, 2 * C, True, x[step].astype(F32))
        put(xc, 0, PIX, C, 2 * C, True, sb[...])
        piece = count // 3
        v[2 * step] = halo_block(sb[7 * PITCH : 17 * PITCH])
        for i in range(3):
            at = start + i * piece
            ub[at : at + piece] = sigmoid(conv(xc, w, 0, at, piece))
            qb[at : at + piece] = sigmoid(conv(xc, w, 1, at, piece))
        rs = (qb[start : start + count] * sb[start : start + count]).astype(BF).astype(F32)
        v[2 * step + 1] = halo_block(rs[(7 - first) * PITCH : (17 - first) * PITCH])
        put(xc, start, count, C, 2 * C, True, rs)
        start += PITCH
        count -= 2 * PITCH
        piece = count // 3
        for i in range(3):
            at = start + i * piece
            cand = jnp.tanh(conv(xc, w, 2, at, piece))
            u = ub[at : at + piece]
            s = sb[at : at + piece]
            nxt = (1.0 - u) * s + u * cand
            nxt = jnp.where(wide(lab[at : at + piece]) > 0, nxt, 0.0).astype(BF).astype(F32)
            if step == 0:
                lo, hi = max(at, 6 * PITCH), min(at + piece, 18 * PITCH)
                if lo < hi:
                    c0[lo - 6 * PITCH : hi - 6 * PITCH] = cand[lo - at : hi - at]
            else:
                c1[at - 4 * PITCH : at - 4 * PITCH + piece] = cand
                s1[at - 4 * PITCH : at - 4 * PITCH + piece] = s.astype(BF)
            qb_at = at
            sb[qb_at : qb_at + piece] = nxt
        if step == 0:
            u0[...] = ub[6 * PITCH : 18 * PITCH]
            q0[...] = qb[6 * PITCH : 18 * PITCH]
        else:
            u1[...] = ub[4 * PITCH : 20 * PITCH]
            q1[...] = qb[4 * PITCH : 20 * PITCH]
    last = sb[8 * PITCH : 16 * PITCH]
    s2[...] = last.astype(BF)
    rain = jnp.sum(last * ro[...], axis=1, keepdims=True)
    labels = lab[8 * PITCH : 16 * PITCH]
    column = lax.rem(lax.broadcasted_iota(jnp.int32, labels.shape, 0), PITCH)
    labels = jnp.where((column >= RIM) & (column < RIM + OWN_COLS), labels, 0)
    lanes = lax.broadcasted_iota(jnp.int32, labels.shape, 1) + 1
    for i in range(K // 128):
        hit = labels == lanes + 128 * i
        tot[i : i + 1] = jnp.sum(jnp.where(hit, rain, 0.0), axis=0, keepdims=True)
        tot[4 + i : 5 + i] = jnp.sum(jnp.where(hit, 1.0, 0.0), axis=0, keepdims=True)


def adjoint(px, w, gates, start, count):
    total = None
    width = len(gates) * C
    for a in range(3):
        lhs = px[pl.ds(start + (1 - a) * PITCH, count), : 3 * width]
        rhs = jnp.concatenate(
            [w[:, g, 3 * a + b, :, C:].reshape(C, C) for b in range(3) for g in gates], axis=0
        )
        term = jnp.dot(lhs, rhs, preferred_element_type=F32)
        total = term if total is None else total + term
    return total


def backward_kernel(
    tp, tgt, w, lab, ro, u1, q1, c1, s1, u0, q0, c0, s0, s2, msg, loss, px, gs
):
    sums = jnp.sum(tp[...], axis=0)
    scale = 1.0 / (sums[4:8] + 1.0)
    mean = sums[0:4] * scale
    rate = jnp.maximum(mean, 0.0) + jnp.log1p(jnp.exp(-jnp.abs(mean)))
    miss = rate - tgt[...]
    loss[...] = jnp.broadcast_to(0.5 / K * jnp.sum(miss * miss), (8, 128))
    gm = miss * (1.0 / K) * (1.0 / (1.0 + jnp.exp(-mean))) * scale

    labels = lab[4 * PITCH : 20 * PITCH]
    lanes = lax.broadcasted_iota(jnp.int32, labels.shape, 1) + 1
    grain = jnp.zeros(labels.shape, F32)
    for i in range(K // 128):
        grain += jnp.where(labels == lanes + 128 * i, gm[i : i + 1], 0.0)
    grain = jnp.sum(grain, axis=1, keepdims=True)
    gs[4 * PITCH : 20 * PITCH] = grain * ro[...]
    part = s2[...].astype(F32) * grain[4 * PITCH : 12 * PITCH]
    column = lax.rem(lax.broadcasted_iota(jnp.int32, part.shape, 0), PITCH)
    part = jnp.where((column >= RIM) & (column < RIM + OWN_COLS), part, 0.0)
    part = jnp.sum(part, axis=0, keepdims=True)
    part_hi = part.astype(BF).astype(F32)
    tail = lax.broadcasted_iota(jnp.int32, (16, C), 0)
    tail = jnp.where(tail == 0, part_hi, jnp.where(tail == 1, part - part_hi, 0.0)).astype(BF)
    for j in range(8):
        msg[j, 224:240] = tail

    def send(slot, field):
        turned = own_pixels(field).T.astype(BF)
        for j in range(8):
            msg[j, slot * 32 : slot * 32 + 32] = turned[j * 32 : j * 32 + 32]

    for step in (1, 0):
        first = 4 if step == 1 else 6
        rows = ROWS_IN - 2 * first
        uv, qv, cv = (u1, q1, c1) if step == 1 else (u0, q0, c0)

        def state(lo, hi):
            if step == 1:
                return s1[(lo - 4) * PITCH : (hi - 4) * PITCH].astype(F32)
            return s0[lo * PITCH : hi * PITCH].astype(F32)

        def at(ref, lo, hi):
            return ref[(lo - first) * PITCH : (hi - first) * PITCH]

        lo, hi = first, first + rows
        g = gs[lo * PITCH : hi * PITCH]
        cand = cv[...]
        pc = (g * uv[...] * (1.0 - cand * cand)).astype(BF).astype(F32)
        put(px, lo * PITCH, rows * PITCH, 0, C, False, pc)
        send(step * 3 + 2, pc[(8 - lo) * PITCH : (16 - lo) * PITCH])
        lo, hi = lo + 1, hi - 1
        n = (hi - lo) * PITCH
        grs = adjoint(px, w, (2,), lo * PITCH, n)
        s = state(lo, hi)
        g = gs[lo * PITCH : hi * PITCH]
        u, q, cand = at(uv, lo, hi), at(qv, lo, hi), at(cv, lo, hi)
        pu = (g * (cand - s) * u * (1.0 - u)).astype(BF).astype(F32)
        pq = (grs * s * q * (1.0 - q)).astype(BF).astype(F32)
        gs[lo * PITCH : hi * PITCH] = g * (1.0 - u) + grs * q
        put(px, lo * PITCH, n, 0, 2 * C, False, pu)
        put(px, lo * PITCH, n, C, 2 * C, False, pq)
        send(step * 3, pu[(8 - lo) * PITCH : (16 - lo) * PITCH])
        send(step * 3 + 1, pq[(8 - lo) * PITCH : (16 - lo) * PITCH])
        lo, hi = lo + 1, hi - 1
        n = (hi - lo) * PITCH
        g = gs[lo * PITCH : hi * PITCH] + adjoint(px, w, (0, 1), lo * PITCH, n)
        g = jnp.where(wide(lab[lo * PITCH : hi * PITCH]) > 0, g, 0.0)
        if step == 1:
            gs[lo * PITCH : hi * PITCH] = g
        else:
            send(6, g)


def corr_kernel(r, vf, vs, out, p3):
    def lanes_of(j, t):
        return r[j, t * 96 : t * 96 + 96, :].astype(F32)

    column = lax.rem(lax.broadcasted_iota(jnp.int32, (96, OWN), 1), OWN_COLS)
    for t in range(2):
        for j in range(8):
            here = lanes_of(j, t)
            nxt = pltpu.roll(here, OWN - 1, axis=1)
            prv = pltpu.roll(here, 1, axis=1)
            over = pltpu.roll(lanes_of(j + 1, t), OWN_COLS - 1, axis=1) if j < 7 else jnp.zeros_like(here)
            under = pltpu.roll(lanes_of(j - 1, t), OWN - OWN_COLS + 1, axis=1) if j > 0 else jnp.zeros_like(here)
            nxt = jnp.where(column == OWN_COLS - 1, over, nxt)
            prv = jnp.where(column == 0, under, prv)
            at = (t * 8 + j) * OWN
            for b, field in enumerate((nxt, here, prv)):
                for g in range(3):
                    p3[g * 96 + b * 32 : g * 96 + b * 32 + 32, at : at + OWN] = field[
                        g * 32 : g * 32 + 32
                    ].astype(BF)

    def store(g, a, value, half):
        for b in range(3):
            slot = g * 9 + 3 * a + b
            for l in range(2):
                lane = half * 2 + l
                out[lane * 4 + slot // 7, (slot % 7) * 32 : (slot % 7) * 32 + 32] = value[
                    b * 32 : b * 32 + 32, l * 128 : l * 128 + 128
                ].astype(BF)

    order = [(t, j) for t in range(2) for j in range(8)]
    for a in range(3):
        field = jnp.concatenate(
            [vf[t, a : a + 8, j].reshape(OWN, C) for t, j in order], axis=0
        )
        value = jnp.dot(p3[...], field, preferred_element_type=F32)
        for g in range(3):
            store(g, a, value[g * 96 : g * 96 + 96], 0)
        field = jnp.concatenate([vs[j, 2 * t, a * 32 : a * 32 + OWN] for t, j in order], axis=0)
        value = jnp.dot(p3[0:192], field, preferred_element_type=F32)
        for g in range(2):
            store(g, a, value[g * 96 : g * 96 + 96], 1)
        field = jnp.concatenate([vs[j, 2 * t + 1, a * 32 : a * 32 + OWN] for t, j in order], axis=0)
        value = jnp.dot(p3[192:288], field, preferred_element_type=F32)
        store(2, a, value, 1)

    tail = jnp.sum(r[:, 224:240, :].astype(F32), axis=0)
    part = tail[0:1] + tail[1:2]
    part_hi = part.astype(BF).astype(F32)
    row = lax.broadcasted_iota(jnp.int32, (32, C), 0)
    last = jnp.where(row == 0, part_hi, jnp.where(row == 1, part - part_hi, 0.0)).astype(BF)
    for l in range(2):
        out[l * 4 + 3, 192:224] = last[:, l * 128 : l * 128 + 128]
        out[l * 4 + 11, 192:224] = jnp.zeros((32, 128), BF)


def call(kernel, outs, scratch, flops, moved, *args):
    return pl.pallas_call(
        kernel,
        out_shape=outs,
        in_specs=[pl.BlockSpec(memory_space=pltpu.VMEM)] * len(args),
        out_specs=jax.tree.map(lambda _: pl.BlockSpec(memory_space=pltpu.VMEM), outs),
        scratch_shapes=scratch,
        compiler_params=pltpu.CompilerParams(vmem_limit_bytes=VMEM_LIMIT),
        cost_estimate=pl.CostEstimate(flops=flops, bytes_accessed=moved, transcendentals=0),
    )(*args)


def shape(*dims, dtype=F32):
    return jax.ShapeDtypeStruct(dims, dtype)


def columns_window(field, axis, at):
    widths = [(0, 0)] * field.ndim
    widths[axis] = (RIM, RIM)
    return lax.dynamic_slice_in_dim(jnp.pad(field, widths), at, PITCH, axis=axis)


def per_device(frames, hidden_init, gate_weight, readout, catchment, targets):
    chan = lax.axis_index("chan")
    row_tile = lax.axis_index("rows")
    up = [(i, i + 1) for i in range(15)]
    down = [(i + 1, i) for i in range(15)]

    weights = lax.all_gather(jnp.transpose(gate_weight, (0, 2, 1, 3)), "chan", axis=0)

    padded = jnp.pad(hidden_init, ((0, 0), (0, 0), (RIM, RIM)))
    pieces = jnp.stack([padded[:, :, 32 * j : 32 * j + PITCH] for j in range(8)])
    own_readout = jnp.broadcast_to(jnp.pad(readout, (0, 8 * PITCH - 32)), (8, 1, 8 * PITCH))
    pieces = jnp.concatenate([pieces.reshape(8, 32, 8 * PITCH), own_readout], axis=1)
    pieces = lax.all_to_all(pieces, "chan", 0, 0)
    ro = pieces[:, 32, :32].reshape(1, C).astype(F32)
    state = jnp.transpose(pieces[:, :32].reshape(C, 8, PITCH), (1, 2, 0))
    turned = jnp.transpose(frames, (0, 2, 3, 1))
    middle = jnp.concatenate([columns_window(turned, 2, 32 * chan), state[None]], axis=0)
    above = lax.ppermute(middle, "rows", up)
    below = lax.ppermute(middle, "rows", down)
    x = jnp.concatenate([above, middle, below], axis=1).reshape(3, PIX, C)
    frame_above = lax.ppermute(turned[:, 7:8], "rows", up)
    frame_below = lax.ppermute(turned[:, 0:1], "rows", down)
    vf = jnp.concatenate([frame_above, turned, frame_below], axis=1).reshape(2, 10, 8, OWN_COLS, C)
    labels = catchment + 1
    labels = jnp.concatenate(
        [lax.ppermute(labels, "rows", up), labels, lax.ppermute(labels, "rows", down)], axis=0
    )
    labels = columns_window(labels, 1, 32 * chan).reshape(PIX, 1)
    labels = jnp.broadcast_to(labels, (PIX, 128))

    n1, n0 = 16 * PITCH, 12 * PITCH
    u1, q1, c1, s1, u0, q0, c0, s2, v, tot = call(
        forward_kernel,
        (
            shape(n1, C), shape(n1, C), shape(n1, C), shape(n1, C, dtype=BF),
            shape(n0, C), shape(n0, C), shape(n0, C), shape(8 * PITCH, C, dtype=BF),
            shape(4, 10 * OWN_COLS, C, dtype=BF), shape(8, 128),
        ),
        [pltpu.VMEM((PIX, 6 * C), BF)] + [pltpu.VMEM((PIX, C), F32)] * 3,
        13_000_000_000, 20_000_000,
        x, weights, labels, ro,
    )
    vs = lax.all_gather(v, "chan", axis=0)
    tp = lax.all_to_all(jnp.broadcast_to(tot[None], (128, 8, 128)), ("rows", "chan"), 0, 0)
    msg, loss = call(
        backward_kernel,
        (shape(8, 240, C, dtype=BF), shape(8, 128)),
        [pltpu.VMEM((PIX, 6 * C), BF), pltpu.VMEM((PIX, C), F32)],
        4_000_000_000, 20_000_000,
        tp, targets.reshape(4, 128), weights, labels, ro, u1, q1, c1, s1, u0, q0, c0, x[2], s2,
    )
    got = lax.all_to_all(msg, "chan", 0, 0)
    hidden_grad = got[:, 192:224].reshape(8, 32, 8, OWN_COLS)
    hidden_grad = jnp.transpose(hidden_grad, (1, 2, 0, 3)).reshape(32, 8, 8 * OWN_COLS).astype(F32)
    part = call(
        corr_kernel,
        shape(16, 224, 128, dtype=BF),
        [pltpu.VMEM((288, 16 * OWN), BF)],
        4_000_000_000, 10_000_000,
        got, vf, vs,
    )
    mine = lax.all_to_all(part, "rows", 0, 0)
    mine = jnp.sum(mine.astype(F32), axis=0)
    tail = mine[192:193] + mine[193:194]
    tail_hi = tail.astype(BF).astype(F32)
    tail = jnp.concatenate([mine[:192], tail_hi, tail - tail_hi, mine[194:]], axis=0)
    mine = jnp.where(row_tile % 4 == 3, tail, mine).astype(BF)
    whole = lax.all_to_all(jnp.broadcast_to(mine[None], (16, 224, 128)), "rows", 0, 0)
    whole = whole.astype(F32).reshape(4, 4, 7, 32, 128)
    whole = jnp.transpose(whole, (1, 2, 3, 0, 4)).reshape(SLOTS, 32, 2 * C)
    gate_grad = jnp.transpose(whole[:27].reshape(3, 9, 32, 2 * C), (0, 2, 1, 3))
    readout_grad = whole[27, 0, :C] + whole[27, 1, :C]
    readout_grad = lax.dynamic_slice_in_dim(readout_grad, chan * 32, 32)
    return (loss[0, 0], gate_grad, readout_grad, hidden_grad)


def solution(mesh):
    in_specs = (
        P(None, None, "rows", None),
        P("chan", "rows", None),
        P(None, "chan", None, None),
        P("chan"),
        P("rows", None),
        P(),
    )
    out_specs = (P(), P(None, "chan", None, None), P("chan"), P("chan", "rows", None))
    return jax.shard_map(
        per_device, mesh=mesh, in_specs=in_specs, out_specs=out_specs, check_vma=False
    )
```

time: 630 us -> 201 us (0.32); the launches traced: 618 us -> 200 us
  waiting for transfers between devices: 241 us -> 67 us
  matrix products: 160 us -> 0 us
  blocking collectives: 108 us -> 0 us
  Pallas kernels: 0 us -> 42 us
  other arithmetic: 30.6 us -> 8 us
    dot_general x166 -> x0, matrix products: 160 us -> none  [the longest x72 65.5 us: weight_taps(): jnp.einsum('gorw,crw->goc', grad_pre, window, preferred_element_type=jnp....]
    psum x2 -> x0, blocking collectives: 108 us -> none  [the longest x1 65.9 us: per_device(): totals, counts = lax.psum((local_totals, local_counts), ('rows', 'chan'))]
    all_gather x4 -> x2, waiting for transfers between devices: 93.6 us -> 6.88 us  [the longest x1 6.88 us: per_device(): lax.all_gather(jnp.transpose(gate_weight, (0, 2, 1, 3)), 'chan', axis=0)]
    reduce_scatter x4 -> x0, waiting for transfers between devices: 80.1 us -> none  [narrow(): lax.psum_scatter(partial_sum, 'chan', scatter_dimension=0, tiled=True)]
    pallas_call x0 -> x3, Pallas kernels: none -> 42 us  [call(): pl.pallas_call(kernel, out_shape=outs, in_specs=[pl.BlockSpec(memory_spac...]
    all_to_all x0 -> x5, waiting for transfers between devices: none -> 41.1 us  [the longest x1 15.1 us: per_device(): mine = lax.all_to_all(part, 'rows', 0, 0)]
    psum x1 -> x0, waiting for transfers between devices: 31.8 us -> none  [per_device(): gate_grad, readout_grad = lax.psum((gate_part, readout_part), 'rows')]
    all_to_all x0 -> x5, starting transfers between devices: none -> 27.9 us  [the longest x1 8.78 us: per_device(): lax.all_to_all(jnp.broadcast_to(tot[None], (128, 8, 128)), ('rows', 'chan...]
  transfers between devices with their start and end apart: 25 -> 13, of which waited for: 20 -> 10; matrix products, arithmetic and copies ran while one was open for 15% -> 10% of each run, Pallas kernels for 0% -> 7%
where the time goes in v1:
time: 201 us; the launch traced here: 200 us
  waiting for transfers between devices  67 us (33%)
  starting transfers between devices  43.9 us (22%)
  Pallas kernels  42 us (21%)
  local copies, waits for them, and re-layouts  24.7 us (12%)
  between operations  14.4 us (7%)
  other arithmetic  8 us (4%)
    pallas_call x3, Pallas kernels, call(): pl.pallas_call(kernel, out_shape=outs, in_specs=[pl.BlockSpec(memory_spac...  42 us
    all_to_all x1, waiting for transfers between devices, per_device(): mine = lax.all_to_all(part, 'rows', 0, 0)  15.1 us
    all_to_all x1, waiting for transfers between devices, per_device(): lax.all_to_all(jnp.broadcast_to(tot[None], (128, 8, 128)), ('rows', 'chan...  11.6 us
    all_to_all x1, waiting for transfers between devices, per_device(): lax.all_to_all(jnp.broadcast_to(mine[None], (16, 224, 128)), 'rows', 0, 0)  9.79 us
    all_to_all x1, starting transfers between devices, per_device(): lax.all_to_all(jnp.broadcast_to(tot[None], (128, 8, 128)), ('rows', 'chan...  8.78 us
    all_to_all x1, starting transfers between devices, per_device(): mine = lax.all_to_all(part, 'rows', 0, 0)  7.08 us
    all_gather x1, waiting for transfers between devices, per_device(): lax.all_gather(jnp.transpose(gate_weight, (0, 2, 1, 3)), 'chan', axis=0)  6.88 us
    ppermute x1, waiting for transfers between devices, per_device(): lax.ppermute(labels, 'rows', down)  4.97 us
  transfers between devices with their start and end apart: 13, of which 10 were waited for; matrix products, arithmetic and copies ran while one was open for 10% of the time, Pallas kernels for 7%

profile of v1, /device:TPU:0, one launch (start us, length us, event | category | flops | bytes accessed | tf_op | source)
XLA Modules:
  0.0 199.9 jit_solution(12027636421850871682)
XLA Ops:
  7.2 0.0 all-gather.5.cloned.1.call-start
  7.2 0.7 all-gather.5.cloned.1.call-update
  7.9 1.4 pad_slice_fusion
  9.3 0.1 stack.27
  9.4 0.1 stack.28
  9.5 0.1 stack.29
  9.7 0.1 stack.30
  9.8 0.1 stack.31
  9.9 0.1 stack.32
  10.0 0.1 stack.33
  10.1 0.1 stack.34
  10.4 0.7 pad_maximum_fusion.3
  11.1 4.6 %all-to-all-start = ((bf16[8,33,384]{2,1,0:T(8,128)(2,1)}), bf16[8,33,384]{2,1,0:T(8,128)(2,1)S(1)}, u32[]{:S(2)}, u32[]{:S(2)}) async-start(bf16[8,33,384]{2,1,0:T(8,128)(2,1)} %pad_maximum_fusion.3), calls=%async_computation | async-start | bytes 491520 | tf_op jit(solution)/shard_map/all_to_all | solution.py:292
  15.7 3.0 %copy.32 = bf16[2,256,8,256]{1,3,2,0:T(8,128)(2,1)S(1)} copy(bf16[2,256,8,256]{3,2,1,0:T(8,128)(2,1)} %param.6) | data formatting | bytes 4194304 | tf_op args[0]
  18.7 0.1 pad_dynamic-slice_fusion
  18.8 4.2 %all-to-all-done = bf16[8,33,384]{2,1,0:T(8,128)(2,1)S(1)} async-done(((bf16[8,33,384]{2,1,0:T(8,128)(2,1)}), bf16[8,33,384]{2,1,0:T(8,128)(2,1)S(1)}, u32[]{:S(2)}, u32[]{:S(2)}) %all-to-all-start) | async-done | bytes 202784 | tf_op jit(solution)/shard_map/all_to_all | solution.py:292
  23.0 0.4 reshape.109
  23.5 0.3 copy.33
  23.8 0.9 pad_maximum_fusion.2
  24.7 4.7 %collective-permute-start = (bf16[3,8,48,256]{3,2,1,0:T(8,128)(2,1)}, bf16[3,8,48,256]{3,2,1,0:T(8,128)(2,1)}, u32[]{:S(2)}, u32[]{:S(2)}) collective-permute-start(bf16[3,8,48,256]{3,2,1,0:T(8,128)(2,1)} %pad_maximum_fusion.2), channel_id=1, source_target_pairs={{0,8},{8,16},{16,24},{24,32},{32,40},{40,48},{48,56},{56,64},{64,7... | collective-permute-start | bytes 1769480 | tf_op jit(solution)/shard_map/ppermute | solution.py:297
  29.4 1.3 collective-permute-start.1
  30.7 4.5 %collective-permute-start.2 = (s32[8,256]{1,0:T(8,128)S(1)}, s32[8,256]{1,0:T(8,128)S(1)}, u32[]{:S(2)}, u32[]{:S(2)}) collective-permute-start(s32[8,256]{1,0:T(8,128)S(1)} %broadcast_add_fusion), channel_id=1, source_target_pairs={{0,8},{8,16},{16,24},{24,32},{32,40},{40,48},{48,56},{56,64},{64,7... | collective-permute-start | bytes 24584 | tf_op jit(solution)/shard_map/ppermute | solution.py:305
  35.2 1.5 collective-permute-start.3
  36.7 4.4 %collective-permute-done.2 = s32[8,256]{1,0:T(8,128)S(1)} collective-permute-done((s32[8,256]{1,0:T(8,128)S(1)}, s32[8,256]{1,0:T(8,128)S(1)}, u32[]{:S(2)}, u32[]{:S(2)}) %collective-permute-start.2) | collective-permute-done | bytes 8224 | tf_op jit(solution)/shard_map/ppermute | solution.py:305
  41.1 5.0 %collective-permute-done.3 = s32[8,256]{1,0:T(8,128)S(1)} collective-permute-done((s32[8,256]{1,0:T(8,128)S(1)}, s32[8,256]{1,0:T(8,128)S(1)}, u32[]{:S(2)}, u32[]{:S(2)}) %collective-permute-start.3) | collective-permute-done | bytes 8224 | tf_op jit(solution)/shard_map/ppermute | solution.py:305
  46.1 0.1 pad_dynamic-slice_fusion.1
  46.2 0.1 broadcast_in_dim.27
  46.3 0.6 reshape.117.ro
  46.9 2.7 %pad_maximum_fusion.1 = bf16[3,24,48,256]{3,2,1,0:T(8,128)(2,1)} fusion(bf16[3,8,48,256]{3,2,1,0:T(8,128)(2,1)} %collective-permute-done.1, bf16[1,8,48,256]{3,2,1,0:T(8,128)(2,1)S(1)} %copy.33, bf16[2,8,48,256]{3,2,1,0:T(8,128)(2,1)S(1)} %pad_dynamic-slice_fusion, bf16[3,8,48,256]{3,2,1,0:T(8,128)(2,1)} %collective-permute-done), kind=kLoop, calls=%fused_computation.4 | loop fusion | flops 2654208 | bytes 3538944 | tf_op jit(solution)/shard_map/concatenate | solution.py:299
  49.5 6.9 %all-gather.5.cloned.1.call-done = bf16[24,9,32,512]{3,2,1,0:T(8,128)(2,1)} async-done(((bf16[3,9,32,512]{3,2,1,0:T(8,128)(2,1)}), bf16[24,9,32,512]{3,2,1,0:T(8,128)(2,1)}) %all-gather.5.cloned.1.call-update) | async-done | bytes 7077904 | tf_op jit(solution)/shard_map/all_gather | solution.py:286
  56.4 1.0 broadcast_in_dim.28.lab
  57.4 19.5 %shard_map.93 = (f32[768,256]{1,0:T(8,128)}, f32[768,256]{1,0:T(8,128)}, f32[768,256]{1,0:T(8,128)}, bf16[768,256]{1,0:T(8,128)(2,1)}, f32[576,256]{1,0:T(8,128)...) custom-call(bf16[3,1152,256]{2,1,0:T(8,128)(2,1)} %bitcast.29, ...), custom_call_target="tpu_custom_call" | custom-call | flops 12999999488 | bytes 20000000 | tf_op jit(solution)/shard_map/pallas_call | solution.py:259
  77.0 1.5 broadcast_in_dim.29
  78.5 8.8 %all-to-all-start.1 = ((f32[128,8,128]{2,1,0:T(8,128)}), f32[128,8,128]{2,1,0:T(8,128)S(1)}, u32[]{:S(2)}, u32[]{:S(2)}) async-start(f32[128,8,128]{2,1,0:T(8,128)} %broadcast_in_dim.29), calls=%async_computation.1 | async-start | bytes 1048576 | tf_op jit(solution)/shard_map/all_to_all | solution.py:323
  87.3 2.0 slice.97
  89.3 11.6 %all-to-all-done.1.tp = f32[128,8,128]{2,1,0:T(8,128)S(1)} async-done(((f32[128,8,128]{2,1,0:T(8,128)}), f32[128,8,128]{2,1,0:T(8,128)S(1)}, u32[]{:S(2)}, u32[]{:S(2)}) %all-to-all-start.1) | async-done | bytes 524320 | tf_op jit(solution)/shard_map/all_to_all | solution.py:323
  100.8 0.8 copy-done.1
  101.6 13.7 %shard_map.94 = (bf16[8,240,256]{2,1,0:T(8,128)(2,1)}, f32[8,128]{1,0:T(8,128)}) custom-call(f32[128,8,128]{2,1,0:T(8,128)} %copy-done.1, f32[4,128]{1,0:T(4,128)} %bitcast.38, bf16[8,3,9,32,512]{4,3,2,1,0:T(8,128)(2,1)} %bitcast.36, s32[1152,128]{1,0:T(8,128)} %broadcast_in_dim.28.lab, f32[1,256]{1,0:T(1,128)} %reshape.117.ro, ...), custom_call_target="tpu_custom_call" | custom-call | flops 4000000000 | bytes 20000000 | tf_op jit(solution)/shard_map/pallas_call | solution.py:259
  115.4 3.6 %all-to-all-start.2 = ((bf16[8,240,256]{2,1,0:T(8,128)(2,1)}), bf16[8,240,256]{2,1,0:T(8,128)(2,1)S(1)}, u32[]{:S(2)}, u32[]{:S(2)}) async-start(bf16[8,240,256]{2,1,0:T(8,128)(2,1)} %get-tuple-element.26), calls=%async_computation.2 | async-start | bytes 1966080 | tf_op jit(solution)/shard_map/all_to_all | solution.py:331
  119.0 2.7 %collective-permute-start.4 = (bf16[2,1,256,256]{3,2,1,0:T(8,128)(2,1)S(1)}, bf16[2,1,256,256]{3,2,1,0:T(8,128)(2,1)S(1)}, u32[]{:S(2)}, u32[]{:S(2)}) collective-permute-start(bf16[2,1,256,256]{3,2,1,0:T(8,128)(2,1)S(1)} %get-tuple-element.28), channel_id=1, source_target_pairs={{0,8},{8,16},{16,24},{24,32},{32,40},{40,48},{48,56},{56,64},{64,7... | collective-permute-start | bytes 786440 | tf_op jit(solution)/shard_map/ppermute | solution.py:300
  121.7 1.3 collective-permute-start.5
  123.0 4.8 %collective-permute-done.4 = bf16[2,1,256,256]{3,2,1,0:T(8,128)(2,1)S(1)} collective-permute-done((bf16[2,1,256,256]{3,2,1,0:T(8,128)(2,1)S(1)}, bf16[2,1,256,256]{3,2,1,0:T(8,128)(2,1)S(1)}, u32[]{:S(2)}, u32[]{:S(2)}) %collective-permute-start.4) | collective-permute-done | bytes 262176 | tf_op jit(solution)/shard_map/ppermute | solution.py:300
  127.8 4.1 %collective-permute-done.5 = bf16[2,1,256,256]{3,2,1,0:T(8,128)(2,1)S(1)} collective-permute-done((bf16[2,1,256,256]{3,2,1,0:T(8,128)(2,1)S(1)}, bf16[2,1,256,256]{3,2,1,0:T(8,128)(2,1)S(1)}, u32[]{:S(2)}, u32[]{:S(2)}) %collective-permute-start.5) | collective-permute-done | bytes 262176 | tf_op jit(solution)/shard_map/ppermute | solution.py:301
  131.9 1.8 pad_maximum_fusion
  133.8 0.4 all-to-all-done.2.r
  134.1 0.9 copy-done
  135.1 8.8 %shard_map.95 = bf16[16,224,128]{2,1,0:T(8,128)(2,1)} custom-call(bf16[8,240,256]{2,1,0:T(8,128)(2,1)} %copy-done, bf16[2,10,8,32,256]{4,3,2,1,0:T(8,128)(2,1)} %bitcast.30, bf16[8,4,320,256]{3,2,1,0:T(8,128)(2,1)} %bitcast.37), custom_call_target="tpu_custom_call" | custom-call | flops 4000000000 | bytes 10000000 | tf_op jit(solution)/shard_map/pallas_call | solution.py:259
  143.8 7.1 %all-to-all-start.3 = ((bf16[16,224,128]{2,1,0:T(8,128)(2,1)}), bf16[16,224,128]{2,1,0:T(8,128)(2,1)S(1)}, u32[]{:S(2)}, u32[]{:S(2)}) async-start(bf16[16,224,128]{2,1,0:T(8,128)(2,1)} %shard_map.95), calls=%async_computation.3 | async-start | bytes 1835008 | tf_op jit(solution)/shard_map/all_to_all | solution.py:341
  150.9 15.1 %all-to-all-done.3 = bf16[16,224,128]{2,1,0:T(8,128)(2,1)S(1)} async-done(((bf16[16,224,128]{2,1,0:T(8,128)(2,1)}), bf16[16,224,128]{2,1,0:T(8,128)(2,1)S(1)}, u32[]{:S(2)}, u32[]{:S(2)}) %all-to-all-start.3) | async-done | bytes 917536 | tf_op jit(solution)/shard_map/all_to_all | solution.py:341
  166.1 0.1 convert_reduce_fusion
  166.3 1.1 broadcast_in_dim.30
  167.3 3.9 %all-to-all-start.4 = ((bf16[16,224,128]{2,1,0:T(8,128)(2,1)}), bf16[16,224,128]{2,1,0:T(8,128)(2,1)S(1)}, u32[]{:S(2)}, u32[]{:S(2)}) async-start(bf16[16,224,128]{2,1,0:T(8,128)(2,1)} %broadcast_in_dim.30), calls=%async_computation.4 | async-start | bytes 1835008 | tf_op jit(solution)/shard_map/all_to_all | solution.py:347
  171.3 1.2 slice.84
  172.4 0.9 slice_convert_fusion
  173.4 0.3 reshape.124
  173.6 0.6 copy.35
  174.3 1.0 reshape.120
  175.3 9.8 %all-to-all-done.4 = bf16[16,224,128]{2,1,0:T(8,128)(2,1)S(1)} async-done(((bf16[16,224,128]{2,1,0:T(8,128)(2,1)}), bf16[16,224,128]{2,1,0:T(8,128)(2,1)S(1)}, u32[]{:S(2)}, u32[]{:S(2)}) %all-to-all-start.4) | async-done | bytes 917536 | tf_op jit(solution)/shard_map/all_to_all | solution.py:347
  185.1 0.2 convert_bitcast_fusion
  185.3 1.5 copy.34
  186.8 2.0 reshape.119
  188.8 0.8 fusion.6
  189.6 2.9 %slice.104 = f32[27,32,512]{2,1,0:T(8,128)} slice(f32[28,32,512]{2,1,0:T(8,128)} %reshape.119), slice={[0:27], [0:32], [0:512]} | slice | bytes 3538944 | tf_op jit(solution)/shard_map/slice | solution.py:350
  192.5 0.6 fusion.3
  (31 shorter events, 0.3 us)
Async XLA Ops:
  7.2 3.0 %copy-start.3 = (bf16[32]{0:T(256)(128)(2,1)S(1)}, bf16[32]{0:T(256)(128)(2,1)}, u32[]{:S(2)}) copy-start(bf16[32]{0:T(256)(128)(2,1)} %param.9) | copy-start | bytes 196
  7.2 49.3 %all-gather.5.cloned.1.call-start = ((), (), s32[]{:S(2)}) async-start(), calls=%async_computation.5 | async-start | bytes 7962624 | tf_op jit(solution)/shard_map/all_gather | solution.py:286
  11.1 11.9 %all-to-all-start = ((bf16[8,33,384]{2,1,0:T(8,128)(2,1)}), bf16[8,33,384]{2,1,0:T(8,128)(2,1)S(1)}, u32[]{:S(2)}, u32[]{:S(2)}) async-start(bf16[8,33,384]{2,1,0:T(8,128)(2,1)} %pad_maximum_fusion.3), calls=%async_computation | async-start | bytes 491520 | tf_op jit(solution)/shard_map/all_to_all | solution.py:292
  15.6 118.5 %all-gather.7.cloned.1.call-start = ((), (), s32[]{:S(2)}) async-start(), calls=%async_computation.6 | async-start | bytes 5898240 | tf_op jit(solution)/shard_map/all_gather | solution.py:322
  18.8 11.9 %copy-start.2 = (s32[8,256]{1,0:T(8,128)S(1)}, s32[8,256]{1,0:T(8,128)}, u32[]{:S(2)}) copy-start(s32[8,256]{1,0:T(8,128)} %param.10) | copy-start | bytes 24580
  24.7 22.2 %collective-permute-start = (bf16[3,8,48,256]{3,2,1,0:T(8,128)(2,1)}, bf16[3,8,48,256]{3,2,1,0:T(8,128)(2,1)}, u32[]{:S(2)}, u32[]{:S(2)}) collective-permute-start(bf16[3,8,48,256]{3,2,1,0:T(8,128)(2,1)} %pad_maximum_fusion.2), channel_id=1, source_target_pairs={{0,8},{8,16},{16,24},{24,32},{32,40},{40,48},{48,56},{56,64},{64,7... | collective-permute-start | bytes 1769480 | tf_op jit(solution)/shard_map/ppermute | solution.py:297
  29.4 17.5 %collective-permute-start.1 = (bf16[3,8,48,256]{3,2,1,0:T(8,128)(2,1)}, bf16[3,8,48,256]{3,2,1,0:T(8,128)(2,1)}, u32[]{:S(2)}, u32[]{:S(2)}) collective-permute-start(bf16[3,8,48,256]{3,2,1,0:T(8,128)(2,1)} %pad_maximum_fusion.2), channel_id=1, source_target_pairs={{8,0},{16,8},{24,16},{32,24},{40,32},{48,40},{56,48},{64,56},{72,6... | collective-permute-start | bytes 1769480 | tf_op jit(solution)/shard_map/ppermute | solution.py:298
  30.7 10.4 %collective-permute-start.2 = (s32[8,256]{1,0:T(8,128)S(1)}, s32[8,256]{1,0:T(8,128)S(1)}, u32[]{:S(2)}, u32[]{:S(2)}) collective-permute-start(s32[8,256]{1,0:T(8,128)S(1)} %broadcast_add_fusion), channel_id=1, source_target_pairs={{0,8},{8,16},{16,24},{24,32},{32,40},{40,48},{48,56},{56,64},{64,7... | collective-permute-start | bytes 24584 | tf_op jit(solution)/shard_map/ppermute | solution.py:305
  35.2 10.9 %collective-permute-start.3 = (s32[8,256]{1,0:T(8,128)S(1)}, s32[8,256]{1,0:T(8,128)S(1)}, u32[]{:S(2)}, u32[]{:S(2)}) collective-permute-start(s32[8,256]{1,0:T(8,128)S(1)} %broadcast_add_fusion), channel_id=1, source_target_pairs={{8,0},{16,8},{24,16},{32,24},{40,32},{48,40},{56,48},{64,56},{72,6... | collective-permute-start | bytes 24584 | tf_op jit(solution)/shard_map/ppermute | solution.py:305
  78.5 22.3 %all-to-all-start.1 = ((f32[128,8,128]{2,1,0:T(8,128)}), f32[128,8,128]{2,1,0:T(8,128)S(1)}, u32[]{:S(2)}, u32[]{:S(2)}) async-start(f32[128,8,128]{2,1,0:T(8,128)} %broadcast_in_dim.29), calls=%async_computation.1 | async-start | bytes 1048576 | tf_op jit(solution)/shard_map/all_to_all | solution.py:323
  100.8 0.8 copy-start.1
  115.4 18.7 %all-to-all-start.2 = ((bf16[8,240,256]{2,1,0:T(8,128)(2,1)}), bf16[8,240,256]{2,1,0:T(8,128)(2,1)S(1)}, u32[]{:S(2)}, u32[]{:S(2)}) async-start(bf16[8,240,256]{2,1,0:T(8,128)(2,1)} %get-tuple-element.26), calls=%async_computation.2 | async-start | bytes 1966080 | tf_op jit(solution)/shard_map/all_to_all | solution.py:331
  119.0 8.8 %collective-permute-start.4 = (bf16[2,1,256,256]{3,2,1,0:T(8,128)(2,1)S(1)}, bf16[2,1,256,256]{3,2,1,0:T(8,128)(2,1)S(1)}, u32[]{:S(2)}, u32[]{:S(2)}) collective-permute-start(bf16[2,1,256,256]{3,2,1,0:T(8,128)(2,1)S(1)} %get-tuple-element.28), channel_id=1, source_target_pairs={{0,8},{8,16},{16,24},{24,32},{32,40},{40,48},{48,56},{56,64},{64,7... | collective-permute-start | bytes 786440 | tf_op jit(solution)/shard_map/ppermute | solution.py:300
  121.7 10.3 %collective-permute-start.5 = (bf16[2,1,256,256]{3,2,1,0:T(8,128)(2,1)S(1)}, bf16[2,1,256,256]{3,2,1,0:T(8,128)(2,1)S(1)}, u32[]{:S(2)}, u32[]{:S(2)}) collective-permute-start(bf16[2,1,256,256]{3,2,1,0:T(8,128)(2,1)S(1)} %get-tuple-element.29), channel_id=1, source_target_pairs={{8,0},{16,8},{24,16},{32,24},{40,32},{48,40},{56,48},{64,56},{72,6... | collective-permute-start | bytes 786440 | tf_op jit(solution)/shard_map/ppermute | solution.py:301
  134.1 0.9 copy-start
  143.8 22.2 %all-to-all-start.3 = ((bf16[16,224,128]{2,1,0:T(8,128)(2,1)}), bf16[16,224,128]{2,1,0:T(8,128)(2,1)S(1)}, u32[]{:S(2)}, u32[]{:S(2)}) async-start(bf16[16,224,128]{2,1,0:T(8,128)(2,1)} %shard_map.95), calls=%async_computation.3 | async-start | bytes 1835008 | tf_op jit(solution)/shard_map/all_to_all | solution.py:341
  167.3 17.7 %all-to-all-start.4 = ((bf16[16,224,128]{2,1,0:T(8,128)(2,1)}), bf16[16,224,128]{2,1,0:T(8,128)(2,1)S(1)}, u32[]{:S(2)}, u32[]{:S(2)}) async-start(bf16[16,224,128]{2,1,0:T(8,128)(2,1)} %broadcast_in_dim.30), calls=%async_computation.4 | async-start | bytes 1835008 | tf_op jit(solution)/shard_map/all_to_all | solution.py:347
Sparse Core Ops, SparseCore 0:
  9.7 46.6 all-gather.4
  77.1 41.2 all-gather.6

commit v2 on v1

--- a/solution.py
+++ b/solution.py
@@ -17,12 +17,23 @@
 OWN = 8 * OWN_COLS
 C = 256
 K = 512
-SLOTS = 28
+CUTS = 2
+V_ROWS = 10 * OWN_COLS
+V_ALL = 4 * V_ROWS + 4 * OWN_COLS
 VMEM_LIMIT = 56 * 1024 * 1024
 
 
 def sigmoid(x):
     return 0.5 * jnp.tanh(0.5 * x) + 0.5
+
+
+class Taps:
+    def __init__(self, ref):
+        self.ref = ref
+
+    def rows(self, gate, tap):
+        block = self.ref[:, gate * 9 + tap]
+        return block.reshape(C, block.shape[-1])
 
 
 def put(dst, row, count, lane, stride, left_first, x):
@@ -41,44 +52,62 @@
     return jnp.concatenate([lab, lab], axis=1)
 
 
-def conv(xc, w, gate, start, count):
+def conv(xc, w, gates, start, count):
     total = None
     for a in range(3):
         lhs = xc[pl.ds(start + (a - 1) * PITCH, count), :]
-        rhs = jnp.concatenate([w[:, gate, 3 * a + b].reshape(C, 2 * C) for b in range(3)], axis=1)
+        rhs = [jnp.concatenate([w.rows(g, 3 * a + b) for b in range(3)], axis=1) for g in gates]
+        rhs = jnp.concatenate(rhs, axis=0) if len(rhs) > 1 else rhs[0]
         term = lax.dot_general(lhs, rhs, (((1,), (1,)), ((), ())), preferred_element_type=F32)
         total = term if total is None else total + term
     return total
 
 
 def forward_kernel(
-    x, w, lab, ro, u1, q1, c1, s1, u0, q0, c0, s2, v, tot, xc, ub, qb, sb
+    above, middle, below, lab, ro, kernels,
+    u1, q1, c1, s1, u0, q0, c0, s0, s2, v, tot, w4, xc, ub, qb, sb, sem
 ):
+    copy = pltpu.make_async_copy(kernels, w4, sem)
+    copy.start()
+    w = Taps(w4)
+
+    def window(k):
+        parts = [ref[k * 8 * PITCH : (k + 1) * 8 * PITCH].astype(F32) for ref in (above, middle, below)]
+        return jnp.concatenate(parts, axis=0)
+
     def halo_block(field):
         return field.reshape(10, PITCH, C)[:, RIM : RIM + OWN_COLS].reshape(10 * OWN_COLS, C).astype(BF)
 
-    sb[...] = x[2].astype(F32)
+    for step in range(2):
+        for n, ref in enumerate((above, below)):
+            line = (step * 8 + 7 - 7 * n) * PITCH
+            at = 4 * V_ROWS + (2 * step + n) * OWN_COLS
+            v[at : at + OWN_COLS] = ref[line : line + PITCH].astype(F32)[RIM : RIM + OWN_COLS].astype(BF)
+    sb[...] = window(2)
     for step in range(2):
         first = 1 + 2 * step
         count = (ROWS_IN - 2 * first) * PITCH
         start = first * PITCH
-        put(xc, 0, PIX, 0, 2 * C, True, x[step].astype(F32))
+        put(xc, 0, PIX, 0, 2 * C, True, window(step))
         put(xc, 0, PIX, C, 2 * C, True, sb[...])
-        piece = count // 3
-        v[2 * step] = halo_block(sb[7 * PITCH : 17 * PITCH])
-        for i in range(3):
+        piece = count // CUTS
+        v[2 * step * V_ROWS : (2 * step + 1) * V_ROWS] = halo_block(sb[7 * PITCH : 17 * PITCH])
+        if step == 0:
+            copy.wait()
+        for i in range(CUTS):
             at = start + i * piece
-            ub[at : at + piece] = sigmoid(conv(xc, w, 0, at, piece))
-            qb[at : at + piece] = sigmoid(conv(xc, w, 1, at, piece))
+            both = sigmoid(conv(xc, w, (0, 1), at, piece))
+            ub[at : at + piece] = both[:, :C]
+            qb[at : at + piece] = both[:, C:]
         rs = (qb[start : start + count] * sb[start : start + count]).astype(BF).astype(F32)
-        v[2 * step + 1] = halo_block(rs[(7 - first) * PITCH : (17 - first) * PITCH])
+        v[(2 * step + 1) * V_ROWS : (2 * step + 2) * V_ROWS] = halo_block(rs[(7 - first) * PITCH : (17 - first) * PITCH])
         put(xc, start, count, C, 2 * C, True, rs)
         start += PITCH
         count -= 2 * PITCH
-        piece = count // 3
-        for i in range(3):
+        piece = count // CUTS
+        for i in range(CUTS):
             at = start + i * piece
-            cand = jnp.tanh(conv(xc, w, 2, at, piece))
+            cand = jnp.tanh(conv(xc, w, (2,), at, piece))
             u = ub[at : at + piece]
             s = sb[at : at + piece]
             nxt = (1.0 - u) * s + u * cand
@@ -93,6 +122,7 @@
             qb_at = at
             sb[qb_at : qb_at + piece] = nxt
         if step == 0:
+            s0[...] = window(2)[6 * PITCH : 18 * PITCH].astype(BF)
             u0[...] = ub[6 * PITCH : 18 * PITCH]
             q0[...] = qb[6 * PITCH : 18 * PITCH]
         else:
@@ -105,10 +135,12 @@
     column = lax.rem(lax.broadcasted_iota(jnp.int32, labels.shape, 0), PITCH)
     labels = jnp.where((column >= RIM) & (column < RIM + OWN_COLS), labels, 0)
     lanes = lax.broadcasted_iota(jnp.int32, labels.shape, 1) + 1
+    totals, counts = [], []
     for i in range(K // 128):
         hit = labels == lanes + 128 * i
-        tot[i : i + 1] = jnp.sum(jnp.where(hit, rain, 0.0), axis=0, keepdims=True)
-        tot[4 + i : 5 + i] = jnp.sum(jnp.where(hit, 1.0, 0.0), axis=0, keepdims=True)
+        totals.append(jnp.sum(jnp.where(hit, rain, 0.0), axis=0, keepdims=True))
+        counts.append(jnp.sum(jnp.where(hit, 1.0, 0.0), axis=0, keepdims=True))
+    tot[...] = jnp.broadcast_to(jnp.concatenate(totals + counts, axis=0)[None], tot.shape)
 
 
 def adjoint(px, w, gates, start, count):
@@ -117,7 +149,7 @@
     for a in range(3):
         lhs = px[pl.ds(start + (1 - a) * PITCH, count), : 3 * width]
         rhs = jnp.concatenate(
-            [w[:, g, 3 * a + b, :, C:].reshape(C, C) for b in range(3) for g in gates], axis=0
+            [w.rows(g, 3 * a + b) for b in range(3) for g in gates], axis=0
         )
         term = jnp.dot(lhs, rhs, preferred_element_type=F32)
         total = term if total is None else total + term
@@ -125,8 +157,11 @@
 
 
 def backward_kernel(
-    tp, tgt, w, lab, ro, u1, q1, c1, s1, u0, q0, c0, s0, s2, msg, loss, px, gs
+    tp, tgt, lab, ro, u1, q1, c1, s1, u0, q0, c0, s0, s2, kernels, msg, loss, w4, px, gs, sem
 ):
+    copy = pltpu.make_async_copy(kernels.at[:, :, :, C:], w4, sem)
+    copy.start()
+    w = Taps(w4)
     sums = jnp.sum(tp[...], axis=0)
     scale = 1.0 / (sums[4:8] + 1.0)
     mean = sums[0:4] * scale
@@ -165,7 +200,7 @@
         def state(lo, hi):
             if step == 1:
                 return s1[(lo - 4) * PITCH : (hi - 4) * PITCH].astype(F32)
-            return s0[lo * PITCH : hi * PITCH].astype(F32)
+            return s0[(lo - 6) * PITCH : (hi - 6) * PITCH].astype(F32)
 
         def at(ref, lo, hi):
             return ref[(lo - first) * PITCH : (hi - first) * PITCH]
@@ -178,6 +213,8 @@
         send(step * 3 + 2, pc[(8 - lo) * PITCH : (16 - lo) * PITCH])
         lo, hi = lo + 1, hi - 1
         n = (hi - lo) * PITCH
+        if step == 1:
+            copy.wait()
         grs = adjoint(px, w, (2,), lo * PITCH, n)
         s = state(lo, hi)
         g = gs[lo * PITCH : hi * PITCH]
@@ -199,7 +236,14 @@
             send(6, g)
 
 
-def corr_kernel(r, vf, vs, out, p3):
+def corr_kernel(r, frames, gathered, out, vs, vf, p3, sems):
+    copies = [
+        pltpu.make_async_copy(frames, vf, sems.at[0]),
+        pltpu.make_async_copy(gathered, vs, sems.at[1]),
+    ]
+    for copy in copies:
+        copy.start()
+
     def lanes_of(j, t):
         return r[j, t * 96 : t * 96 + 96, :].astype(F32)
 
@@ -220,6 +264,9 @@
                         g * 32 : g * 32 + 32
                     ].astype(BF)
 
+    for copy in copies:
+        copy.wait()
+
     def store(g, a, value, half):
         for b in range(3):
             slot = g * 9 + 3 * a + b
@@ -229,19 +276,25 @@
                     b * 32 : b * 32 + 32, l * 128 : l * 128 + 128
                 ].astype(BF)
 
+    def frame_rows(t, j, a):
+        at = 4 * V_ROWS + 2 * t * OWN_COLS
+        if a == 0:
+            return vs[j, at : at + OWN_COLS], vf[t, 0:7, j].reshape(7 * OWN_COLS, C)
+        if a == 1:
+            return (vf[t, :, j].reshape(OWN, C),)
+        return vf[t, 1:8, j].reshape(7 * OWN_COLS, C), vs[j, at + OWN_COLS : at + 2 * OWN_COLS]
+
     order = [(t, j) for t in range(2) for j in range(8)]
     for a in range(3):
-        field = jnp.concatenate(
-            [vf[t, a : a + 8, j].reshape(OWN, C) for t, j in order], axis=0
-        )
+        field = jnp.concatenate([part for t, j in order for part in frame_rows(t, j, a)], axis=0)
         value = jnp.dot(p3[...], field, preferred_element_type=F32)
         for g in range(3):
             store(g, a, value[g * 96 : g * 96 + 96], 0)
-        field = jnp.concatenate([vs[j, 2 * t, a * 32 : a * 32 + OWN] for t, j in order], axis=0)
+        field = jnp.concatenate([vs[j, pl.ds(2 * t * V_ROWS + a * OWN_COLS, OWN)] for t, j in order], axis=0)
         value = jnp.dot(p3[0:192], field, preferred_element_type=F32)
         for g in range(2):
             store(g, a, value[g * 96 : g * 96 + 96], 1)
-        field = jnp.concatenate([vs[j, 2 * t + 1, a * 32 : a * 32 + OWN] for t, j in order], axis=0)
+        field = jnp.concatenate([vs[j, pl.ds((2 * t + 1) * V_ROWS + a * OWN_COLS, OWN)] for t, j in order], axis=0)
         value = jnp.dot(p3[192:288], field, preferred_element_type=F32)
         store(2, a, value, 1)
 
@@ -255,14 +308,41 @@
         out[l * 4 + 11, 192:224] = jnp.zeros((32, 128), BF)
 
 
-def call(kernel, outs, scratch, flops, moved, *args):
+def finish_sum_kernel(last, parts, out):
+    total = parts[0].astype(F32)
+    for n in range(1, 16):
+        total = total + parts[n].astype(F32)
+    pair = total[192:193] + total[193:194]
+    pair_hi = pair.astype(BF).astype(F32)
+    row = lax.broadcasted_iota(jnp.int32, total.shape, 0)
+    split = jnp.where(row == 192, pair_hi, jnp.where(row == 193, pair - pair_hi, total))
+    total = jnp.where(last[0] == 1, split, total).astype(BF)
+    out[...] = jnp.broadcast_to(total[None], out.shape)
+
+
+def layout_kernel(parts, grad, readout):
+    for lane in range(4):
+        for group in range(4):
+            block = parts[lane * 4 + group].astype(F32).reshape(7, 32, 128)
+            count = min(7, 27 - group * 7)
+            grad[group * 7 : group * 7 + count, :, lane * 128 : lane * 128 + 128] = block[:count]
+            if group == 3 and lane < 2:
+                readout[:, lane * 128 : lane * 128 + 128] = block[6, 0:1] + block[6, 1:2]
+
+
+VM = pl.BlockSpec(memory_space=pltpu.VMEM)
+SM = pl.BlockSpec(memory_space=pltpu.SMEM)
+HB = pl.BlockSpec(memory_space=pl.ANY)
+
+
+def call(kernel, specs, outs, scratch, flops, moved, *args, limit=VMEM_LIMIT):
     return pl.pallas_call(
         kernel,
         out_shape=outs,
-        in_specs=[pl.BlockSpec(memory_space=pltpu.VMEM)] * len(args),
-        out_specs=jax.tree.map(lambda _: pl.BlockSpec(memory_space=pltpu.VMEM), outs),
+        in_specs=specs,
+        out_specs=jax.tree.map(lambda _: VM, outs),
         scratch_shapes=scratch,
-        compiler_params=pltpu.CompilerParams(vmem_limit_bytes=VMEM_LIMIT),
+        compiler_params=pltpu.CompilerParams(vmem_limit_bytes=limit),
         cost_estimate=pl.CostEstimate(flops=flops, bytes_accessed=moved, transcendentals=0),
     )(*args)
 
@@ -283,73 +363,78 @@
     up = [(i, i + 1) for i in range(15)]
     down = [(i + 1, i) for i in range(15)]
 
-    weights = lax.all_gather(jnp.transpose(gate_weight, (0, 2, 1, 3)), "chan", axis=0)
-
     padded = jnp.pad(hidden_init, ((0, 0), (0, 0), (RIM, RIM)))
     pieces = jnp.stack([padded[:, :, 32 * j : 32 * j + PITCH] for j in range(8)])
     own_readout = jnp.broadcast_to(jnp.pad(readout, (0, 8 * PITCH - 32)), (8, 1, 8 * PITCH))
     pieces = jnp.concatenate([pieces.reshape(8, 32, 8 * PITCH), own_readout], axis=1)
+    own_kernel = jnp.transpose(gate_weight, (0, 2, 1, 3)).reshape(27, 32, 2 * C)
+    kernels = lax.all_gather(own_kernel, "chan", axis=0)
     pieces = lax.all_to_all(pieces, "chan", 0, 0)
+    turned = jnp.transpose(frames, (0, 2, 3, 1))
     ro = pieces[:, 32, :32].reshape(1, C).astype(F32)
-    state = jnp.transpose(pieces[:, :32].reshape(C, 8, PITCH), (1, 2, 0))
-    turned = jnp.transpose(frames, (0, 2, 3, 1))
-    middle = jnp.concatenate([columns_window(turned, 2, 32 * chan), state[None]], axis=0)
+    state = jnp.transpose(pieces[:, :32].reshape(C, 8 * PITCH))
+    labels = columns_window(catchment + 1, 1, 32 * chan).reshape(-1)
+    digits = jnp.concatenate([labels // 256, labels % 256]).astype(BF).reshape(3, C)
+    middle = columns_window(turned, 2, 32 * chan).reshape(16 * PITCH, C)
+    middle = jnp.concatenate([middle, state, jnp.pad(digits, ((0, 13), (0, 0)))], axis=0)
     above = lax.ppermute(middle, "rows", up)
     below = lax.ppermute(middle, "rows", down)
-    x = jnp.concatenate([above, middle, below], axis=1).reshape(3, PIX, C)
-    frame_above = lax.ppermute(turned[:, 7:8], "rows", up)
-    frame_below = lax.ppermute(turned[:, 0:1], "rows", down)
-    vf = jnp.concatenate([frame_above, turned, frame_below], axis=1).reshape(2, 10, 8, OWN_COLS, C)
-    labels = catchment + 1
-    labels = jnp.concatenate(
-        [lax.ppermute(labels, "rows", up), labels, lax.ppermute(labels, "rows", down)], axis=0
-    )
-    labels = columns_window(labels, 1, 32 * chan).reshape(PIX, 1)
+    digits = jnp.stack([part[24 * PITCH : 24 * PITCH + 3] for part in (above, middle, below)])
+    digits = digits.reshape(3, 2, 8 * PITCH).astype(jnp.int32)
+    labels = (digits[:, 0] * 256 + digits[:, 1]).reshape(PIX, 1)
     labels = jnp.broadcast_to(labels, (PIX, 128))
 
     n1, n0 = 16 * PITCH, 12 * PITCH
-    u1, q1, c1, s1, u0, q0, c0, s2, v, tot = call(
+    dma = pltpu.SemaphoreType.DMA(())
+    u1, q1, c1, s1, u0, q0, c0, s0, s2, v, tot = call(
         forward_kernel,
+        [VM] * 5 + [HB],
         (
             shape(n1, C), shape(n1, C), shape(n1, C), shape(n1, C, dtype=BF),
-            shape(n0, C), shape(n0, C), shape(n0, C), shape(8 * PITCH, C, dtype=BF),
-            shape(4, 10 * OWN_COLS, C, dtype=BF), shape(8, 128),
+            shape(n0, C), shape(n0, C), shape(n0, C), shape(n0, C, dtype=BF), shape(8 * PITCH, C, dtype=BF),
+            shape(V_ALL, C, dtype=BF), shape(128, 8, 128),
         ),
-        [pltpu.VMEM((PIX, 6 * C), BF)] + [pltpu.VMEM((PIX, C), F32)] * 3,
+        [pltpu.VMEM((8, 27, 32, 2 * C), BF), pltpu.VMEM((PIX, 6 * C), BF)] + [pltpu.VMEM((PIX, C), F32)] * 3 + [dma],
         13_000_000_000, 20_000_000,
-        x, weights, labels, ro,
-    )
+        above, middle, below, labels, ro, kernels,
+    )
+    tp = lax.all_to_all(tot, ("rows", "chan"), 0, 0)
     vs = lax.all_gather(v, "chan", axis=0)
-    tp = lax.all_to_all(jnp.broadcast_to(tot[None], (128, 8, 128)), ("rows", "chan"), 0, 0)
     msg, loss = call(
         backward_kernel,
+        [VM] * 13 + [HB],
         (shape(8, 240, C, dtype=BF), shape(8, 128)),
-        [pltpu.VMEM((PIX, 6 * C), BF), pltpu.VMEM((PIX, C), F32)],
+        [pltpu.VMEM((8, 27, 32, C), BF), pltpu.VMEM((PIX, 6 * C), BF), pltpu.VMEM((PIX, C), F32), dma],
         4_000_000_000, 20_000_000,
-        tp, targets.reshape(4, 128), weights, labels, ro, u1, q1, c1, s1, u0, q0, c0, x[2], s2,
+        tp, targets.reshape(4, 128), labels, ro, u1, q1, c1, s1, u0, q0, c0, s0, s2, kernels,
     )
     got = lax.all_to_all(msg, "chan", 0, 0)
     hidden_grad = got[:, 192:224].reshape(8, 32, 8, OWN_COLS)
     hidden_grad = jnp.transpose(hidden_grad, (1, 2, 0, 3)).reshape(32, 8, 8 * OWN_COLS).astype(F32)
     part = call(
         corr_kernel,
+        [VM, HB, HB],
         shape(16, 224, 128, dtype=BF),
-        [pltpu.VMEM((288, 16 * OWN), BF)],
+        [
+            pltpu.VMEM((8, V_ALL, C), BF), pltpu.VMEM((2, 8, 8, OWN_COLS, C), BF),
+            pltpu.VMEM((288, 16 * OWN), BF), pltpu.SemaphoreType.DMA((2,)),
+        ],
         4_000_000_000, 10_000_000,
-        got, vf, vs,
+        got, turned.reshape(2, 8, 8, OWN_COLS, C), vs,
     )
     mine = lax.all_to_all(part, "rows", 0, 0)
-    mine = jnp.sum(mine.astype(F32), axis=0)
-    tail = mine[192:193] + mine[193:194]
-    tail_hi = tail.astype(BF).astype(F32)
-    tail = jnp.concatenate([mine[:192], tail_hi, tail - tail_hi, mine[194:]], axis=0)
-    mine = jnp.where(row_tile % 4 == 3, tail, mine).astype(BF)
-    whole = lax.all_to_all(jnp.broadcast_to(mine[None], (16, 224, 128)), "rows", 0, 0)
-    whole = whole.astype(F32).reshape(4, 4, 7, 32, 128)
-    whole = jnp.transpose(whole, (1, 2, 3, 0, 4)).reshape(SLOTS, 32, 2 * C)
-    gate_grad = jnp.transpose(whole[:27].reshape(3, 9, 32, 2 * C), (0, 2, 1, 3))
-    readout_grad = whole[27, 0, :C] + whole[27, 1, :C]
-    readout_grad = lax.dynamic_slice_in_dim(readout_grad, chan * 32, 32)
+    last = (row_tile % 4 == 3).astype(jnp.int32)[None]
+    mine = call(
+        finish_sum_kernel, [SM, VM], shape(16, 224, 128, dtype=BF), [], 1_000_000, 2_000_000, last, mine,
+        limit=16 * 1024 * 1024,
+    )
+    whole = lax.all_to_all(mine, "rows", 0, 0)
+    gate_grad, readout_grad = call(
+        layout_kernel, [VM], (shape(27, 32, 2 * C), shape(1, C)), [], 1_000_000, 3_000_000, whole,
+        limit=16 * 1024 * 1024,
+    )
+    gate_grad = jnp.transpose(gate_grad.reshape(3, 9, 32, 2 * C), (0, 2, 1, 3))
+    readout_grad = lax.dynamic_slice_in_dim(readout_grad[0], chan * 32, 32)
     return (loss[0, 0], gate_grad, readout_grad, hidden_grad)
 
 

time: 201 us -> 191 us (0.950)
  blocking collectives: 0 us -> 22.5 us
  starting transfers between devices: 43.9 us -> 21.9 us
  local copies, waits for them, and re-layouts: 24.7 us -> 15.3 us
  other arithmetic: 8 us -> 2.5 us
  Pallas kernels: 42 us -> 45 us
    all_to_all x0 -> x1, blocking collectives: none -> 22.5 us  [per_device(): tp = lax.all_to_all(tot, ('rows', 'chan'), 0, 0)]
    ppermute x4 -> x0, waiting for transfers between devices: 18.3 us -> none  [the longest x1 4.97 us: per_device(): lax.ppermute(labels, 'rows', down)]
    all_to_all x1, waiting for transfers between devices: 0.38 us -> 12.4 us  [per_device(): got = lax.all_to_all(msg, 'chan', 0, 0)]
    all_to_all x2 -> x1, waiting for transfers between devices: 21.4 us -> 10.1 us  [per_device(): whole = lax.all_to_all(mine, 'rows', 0, 0)]
    ppermute x4 -> x0, starting transfers between devices: 9.99 us -> none  [the longest x1 4.55 us: per_device(): lax.ppermute(labels, 'rows', up)]
    all_to_all x2 -> x1, starting transfers between devices: 12.7 us -> 3.63 us  [per_device(): whole = lax.all_to_all(mine, 'rows', 0, 0)]
    ppermute x1, waiting for transfers between devices: 0.01 us -> 8.75 us  [per_device(): above = lax.ppermute(middle, 'rows', up)]
    concatenate x4 -> x1, other arithmetic: 5.35 us -> 0.04 us  [per_device(): jnp.concatenate([middle, state, jnp.pad(digits, ((0, 13), (0, 0)))], axis=0)]
  transfers between devices with their start and end apart: 13 -> 8, of which waited for: 10 -> 7; matrix products, arithmetic and copies ran while one was open for 10% -> 8% of each run, Pallas kernels for 7% -> 7%
where the time goes in v2:
time: 191 us; the launch traced here: 190 us
  waiting for transfers between devices  68.6 us (36%)
  Pallas kernels  45 us (24%)
  blocking collectives  22.5 us (12%)
  starting transfers between devices  21.9 us (11%)
  local copies, waits for them, and re-layouts  15.3 us (8%)
  between operations  14.3 us (7%)
  other arithmetic  2.5 us (1%)
    pallas_call x5, Pallas kernels, call(): pl.pallas_call(kernel, out_shape=outs, in_specs=specs, out_specs=jax.tree...  45 us
    all_to_all x1, blocking collectives, per_device(): tp = lax.all_to_all(tot, ('rows', 'chan'), 0, 0)  22.5 us
    all_to_all x1, waiting for transfers between devices, per_device(): mine = lax.all_to_all(part, 'rows', 0, 0)  16.2 us
    all_to_all x1, waiting for transfers between devices, per_device(): got = lax.all_to_all(msg, 'chan', 0, 0)  12.4 us
    all_to_all x1, waiting for transfers between devices, per_device(): whole = lax.all_to_all(mine, 'rows', 0, 0)  10.1 us
    all_gather x1, waiting for transfers between devices, per_device(): kernels = lax.all_gather(own_kernel, 'chan', axis=0)  10.1 us
    ppermute x1, waiting for transfers between devices, per_device(): above = lax.ppermute(middle, 'rows', up)  8.75 us
    all_to_all x1, waiting for transfers between devices, per_device(): pieces = lax.all_to_all(pieces, 'chan', 0, 0)  6.05 us
  transfers between devices with their start and end apart: 8, of which 7 were waited for; matrix products, arithmetic and copies ran while one was open for 8% of the time, Pallas kernels for 7%

profile of v2, /device:TPU:0, one launch (start us, length us, event | category | flops | bytes accessed | tf_op | source)
XLA Modules:
  0.0 190.0 jit_solution(8165832376955882081)
XLA Ops:
  7.2 0.0 copy-start.4
  7.2 0.0 all-gather.4.cloned.1.call-start
  7.2 0.7 all-gather.4.cloned.1.call-update
  7.9 0.0 copy-start.3
  7.9 0.0 copy-start
  7.9 1.5 pad_slice_fusion
  9.4 0.1 stack.37
  9.5 0.1 stack.38
  9.6 0.1 stack.39
  9.7 0.1 stack.40
  9.8 0.1 stack.41
  10.0 0.1 stack.42
  10.1 0.1 stack.43
  10.2 0.1 stack.44
  10.3 0.0 copy-done.4
  10.4 0.7 pad_maximum_fusion
  11.2 4.6 %all-to-all-start = ((bf16[8,33,384]{2,1,0:T(8,128)(2,1)}), bf16[8,33,384]{2,1,0:T(8,128)(2,1)}, u32[]{:S(2)}, u32[]{:S(2)}) async-start(bf16[8,33,384]{2,1,0:T(8,128)(2,1)} %pad_maximum_fusion), calls=%async_computation | async-start | bytes 491520 | tf_op jit(solution)/shard_map/all_to_all | solution.py:372
  15.7 0.0 all-gather.6.cloned.1.call-start
  15.8 0.0 copy-done.3
  15.8 0.1 pad_dynamic-slice_fusion.1
  15.9 0.1 reshape.102
  16.0 0.0 copy-done
  16.0 0.5 pad_dynamic-slice_fusion
  16.5 0.6 copy.26
  17.1 6.1 %all-to-all-done = bf16[8,33,384]{2,1,0:T(8,128)(2,1)} async-done(((bf16[8,33,384]{2,1,0:T(8,128)(2,1)}), bf16[8,33,384]{2,1,0:T(8,128)(2,1)}, u32[]{:S(2)}, u32[]{:S(2)}) %all-to-all-start) | async-done | bytes 202784 | tf_op jit(solution)/shard_map/all_to_all | solution.py:372
  23.2 1.0 slice.71
  24.2 0.1 copy.27
  24.4 0.0 copy-start.2
  24.4 4.6 %collective-permute-start = (bf16[1168,256]{1,0:T(8,128)(2,1)S(1)}, bf16[1168,256]{1,0:T(8,128)(2,1)}, u32[]{:S(2)}, u32[]{:S(2)}) collective-permute-start(bf16[1168,256]{1,0:T(8,128)(2,1)S(1)} %fusion.1.middle), channel_id=1, source_target_pairs={{0,8},{8,16},{16,24},{24,32},{32,40},{40,48},{48,56},{56,64},{64,7... | collective-permute-start | bytes 1794056 | tf_op jit(solution)/shard_map/ppermute | solution.py:380
  29.0 1.5 collective-permute-start.1
  30.5 0.7 fusion.3
  31.2 0.6 reshape.106.ro
  31.8 8.8 %collective-permute-done.above = bf16[1168,256]{1,0:T(8,128)(2,1)} collective-permute-done((bf16[1168,256]{1,0:T(8,128)(2,1)S(1)}, bf16[1168,256]{1,0:T(8,128)(2,1)}, u32[]{:S(2)}, u32[]{:S(2)}) %collective-permute-start) | collective-permute-done | bytes 598048 | tf_op jit(solution)/shard_map/ppermute | solution.py:380
  40.6 0.7 slice.72
  41.3 4.3 %collective-permute-done.1.below = bf16[1168,256]{1,0:T(8,128)(2,1)} collective-permute-done((bf16[1168,256]{1,0:T(8,128)(2,1)S(1)}, bf16[1168,256]{1,0:T(8,128)(2,1)}, u32[]{:S(2)}, u32[]{:S(2)}) %collective-permute-start.1) | collective-permute-done | bytes 598048 | tf_op jit(solution)/shard_map/ppermute | solution.py:381
  45.6 0.7 slice.73
  46.4 10.1 %all-gather.4.cloned.1.call-done.kernels = bf16[8,27,32,512]{3,2,1,0:T(8,128)(2,1)} async-done(((bf16[1,27,32,512]{3,2,1,0:T(8,128)(2,1)}), bf16[8,27,32,512]{3,2,1,0:T(8,128)(2,1)}) %all-gather.4.cloned.1.call-update) | async-done | bytes 7077904 | tf_op jit(solution)/shard_map/all_gather | solution.py:371
  56.4 1.0 broadcast_in_dim.14.lab
  57.5 0.0 copy-done.2
  57.5 19.8 %shard_map.93 = (f32[768,256]{1,0:T(8,128)}, f32[768,256]{1,0:T(8,128)}, f32[768,256]{1,0:T(8,128)}, bf16[768,256]{1,0:T(8,128)(2,1)}, f32[576,256]{1,0:T(8,128)...) custom-call(bf16[1168,256]{1,0:T(8,128)(2,1)} %collective-permute-do, ...), custom_call_target="tpu_custom_call" | custom-call | flops 12999999488 | bytes 20000000 | tf_op jit(solution)/shard_map/pallas_call | solution.py:339
  77.3 0.0 all-gather.6.cloned.1.call-update
  77.3 22.5 %all_to_all.25.tp = f32[128,8,128]{2,1,0:T(8,128)} all-to-all(f32[128,8,128]{2,1,0:T(8,128)} %get-tuple-element.19), channel_id=1, replica_groups=mesh['rows'=16,'chan'=8] {'rows','chan'}, dimensions={0} | all-to-all | bytes 1048576 | tf_op jit(solution)/shard_map/all_to_all | solution.py:401
  99.8 13.1 %shard_map.94 = (bf16[8,240,256]{2,1,0:T(8,128)(2,1)}, f32[8,128]{1,0:T(8,128)}) custom-call(f32[128,8,128]{2,1,0:T(8,128)} %all_to_all.25.tp, f32[4,128]{1,0:T(4,128)} %bitcast.30, s32[1152,128]{1,0:T(8,128)} %broadcast_in_dim.14.lab, f32[1,256]{1,0:T(1,128)} %reshape.106.ro, f32[768,256]{1,0:T(8,128)} %get-tuple-element.20.u1, ...), custom_call_target="tpu_custom_call" | custom-call | flops 4000000000 | bytes 20000000 | tf_op jit(solution)/shard_map/pallas_call | solution.py:339
  112.9 3.6 %all-to-all-start.2 = ((bf16[8,240,256]{2,1,0:T(8,128)(2,1)}), bf16[8,240,256]{2,1,0:T(8,128)(2,1)S(1)}, u32[]{:S(2)}, u32[]{:S(2)}) async-start(bf16[8,240,256]{2,1,0:T(8,128)(2,1)} %get-tuple-element.30), calls=%async_computation.2 | async-start | bytes 1966080 | tf_op jit(solution)/shard_map/all_to_all | solution.py:411
  116.4 2.8 %copy.28 = bf16[2,8,256,256]{3,2,1,0:T(8,128)(2,1)} copy(bf16[2,8,256,256]{2,1,3,0:T(8,128)(2,1)S(1)} %bitcast.21) | data formatting | bytes 4194304 | tf_op jit(solution)/shard_map/transpose | solution.py:373
  119.2 12.4 %all-to-all-done.2.r = bf16[8,240,256]{2,1,0:T(8,128)(2,1)S(1)} async-done(((bf16[8,240,256]{2,1,0:T(8,128)(2,1)}), bf16[8,240,256]{2,1,0:T(8,128)(2,1)S(1)}, u32[]{:S(2)}, u32[]{:S(2)}) %all-to-all-start.2) | async-done | bytes 983072 | tf_op jit(solution)/shard_map/all_to_all | solution.py:411
  131.6 0.0 copy-start.1
  131.6 0.0 all-gather.6.cloned.1.call-done
  131.6 0.9 copy-done.1
  132.6 9.6 %shard_map.95 = bf16[16,224,128]{2,1,0:T(8,128)(2,1)} custom-call(bf16[8,240,256]{2,1,0:T(8,128)(2,1)} %copy-done.1, bf16[2,8,8,32,256]{4,3,2,1,0:T(8,128)(2,1)} %bitcast.23, bf16[8,1408,256]{2,1,0:T(8,128)(2,1)} %bitcast.28), custom_call_target="tpu_custom_call" | custom-call | flops 4000000000 | bytes 10000000 | tf_op jit(solution)/shard_map/pallas_call | solution.py:339
  142.2 3.9 %all-to-all-start.3 = ((bf16[16,224,128]{2,1,0:T(8,128)(2,1)}), bf16[16,224,128]{2,1,0:T(8,128)(2,1)S(1)}, u32[]{:S(2)}, u32[]{:S(2)}) async-start(bf16[16,224,128]{2,1,0:T(8,128)(2,1)} %shard_map.95), calls=%async_computation.3 | async-start | bytes 1835008 | tf_op jit(solution)/shard_map/all_to_all | solution.py:425
  146.1 16.2 %all-to-all-done.3.parts = bf16[16,224,128]{2,1,0:T(8,128)(2,1)S(1)} async-done(((bf16[16,224,128]{2,1,0:T(8,128)(2,1)}), bf16[16,224,128]{2,1,0:T(8,128)(2,1)S(1)}, u32[]{:S(2)}, u32[]{:S(2)}) %all-to-all-start.3) | async-done | bytes 917536 | tf_op jit(solution)/shard_map/all_to_all | solution.py:425
  162.3 1.1 shard_map.96
  163.4 3.6 %all-to-all-start.4 = ((bf16[16,224,128]{2,1,0:T(8,128)(2,1)}), bf16[16,224,128]{2,1,0:T(8,128)(2,1)S(1)}, u32[]{:S(2)}, u32[]{:S(2)}) async-start(bf16[16,224,128]{2,1,0:T(8,128)(2,1)} %shard_map.96), calls=%async_computation.4 | async-start | bytes 1835008 | tf_op jit(solution)/shard_map/all_to_all | solution.py:431
  167.0 1.2 slice.69
  168.2 0.9 slice_convert_fusion
  169.1 0.3 reshape.109
  169.4 0.6 copy.29
  170.0 1.0 reshape.108
  171.0 10.1 %all-to-all-done.4.parts = bf16[16,224,128]{2,1,0:T(8,128)(2,1)S(1)} async-done(((bf16[16,224,128]{2,1,0:T(8,128)(2,1)}), bf16[16,224,128]{2,1,0:T(8,128)(2,1)S(1)}, u32[]{:S(2)}, u32[]{:S(2)}) %all-to-all-start.4) | async-done | bytes 917536 | tf_op jit(solution)/shard_map/all_to_all | solution.py:431
  181.1 1.4 shard_map.97
  182.6 0.6 fusion.5
  (21 shorter events, 0.3 us)
Async XLA Ops:
  7.2 3.1 %copy-start.4 = (bf16[32]{0:T(256)(128)(2,1)S(1)}, bf16[32]{0:T(256)(128)(2,1)}, u32[]{:S(2)}) copy-start(bf16[32]{0:T(256)(128)(2,1)} %param.9) | copy-start | bytes 196
  7.2 49.3 %all-gather.4.cloned.1.call-start = ((), (), s32[]{:S(2)}) async-start(), calls=%async_computation.5 | async-start | bytes 7962624 | tf_op jit(solution)/shard_map/all_gather | solution.py:371
  7.9 7.9 %copy-start.3 = (s32[8,256]{1,0:T(8,128)S(1)}, s32[8,256]{1,0:T(8,128)}, u32[]{:S(2)}) copy-start(s32[8,256]{1,0:T(8,128)} %param.10) | copy-start | bytes 24580
  7.9 8.1 %copy-start = (bf16[2,256,8,256]{3,2,1,0:T(8,128)(2,1)S(1)}, bf16[2,256,8,256]{3,2,1,0:T(8,128)(2,1)}, u32[]{:S(2)}) copy-start(bf16[2,256,8,256]{3,2,1,0:T(8,128)(2,1)} %param.6) | copy-start | bytes 6291460
  11.2 12.0 %all-to-all-start = ((bf16[8,33,384]{2,1,0:T(8,128)(2,1)}), bf16[8,33,384]{2,1,0:T(8,128)(2,1)}, u32[]{:S(2)}, u32[]{:S(2)}) async-start(bf16[8,33,384]{2,1,0:T(8,128)(2,1)} %pad_maximum_fusion), calls=%async_computation | async-start | bytes 491520 | tf_op jit(solution)/shard_map/all_to_all | solution.py:372
  15.7 115.9 %all-gather.6.cloned.1.call-start = ((), (), s32[]{:S(2)}) async-start(), calls=%async_computation.6 | async-start | bytes 6488064 | tf_op jit(solution)/shard_map/all_gather | solution.py:402
  24.4 33.1 %copy-start.2 = (bf16[1168,256]{1,0:T(8,128)(2,1)}, bf16[1168,256]{1,0:T(8,128)(2,1)S(1)}, u32[]{:S(2)}) copy-start(bf16[1168,256]{1,0:T(8,128)(2,1)S(1)} %fusion.1.middle) | copy-start | bytes 1794052
  24.4 16.2 %collective-permute-start = (bf16[1168,256]{1,0:T(8,128)(2,1)S(1)}, bf16[1168,256]{1,0:T(8,128)(2,1)}, u32[]{:S(2)}, u32[]{:S(2)}) collective-permute-start(bf16[1168,256]{1,0:T(8,128)(2,1)S(1)} %fusion.1.middle), channel_id=1, source_target_pairs={{0,8},{8,16},{16,24},{24,32},{32,40},{40,48},{48,56},{56,64},{64,7... | collective-permute-start | bytes 1794056 | tf_op jit(solution)/shard_map/ppermute | solution.py:380
  29.0 16.6 %collective-permute-start.1 = (bf16[1168,256]{1,0:T(8,128)(2,1)S(1)}, bf16[1168,256]{1,0:T(8,128)(2,1)}, u32[]{:S(2)}, u32[]{:S(2)}) collective-permute-start(bf16[1168,256]{1,0:T(8,128)(2,1)S(1)} %fusion.1.middle), channel_id=1, source_target_pairs={{8,0},{16,8},{24,16},{32,24},{40,32},{48,40},{56,48},{64,56},{72,6... | collective-permute-start | bytes 1794056 | tf_op jit(solution)/shard_map/ppermute | solution.py:381
  112.9 18.8 %all-to-all-start.2 = ((bf16[8,240,256]{2,1,0:T(8,128)(2,1)}), bf16[8,240,256]{2,1,0:T(8,128)(2,1)S(1)}, u32[]{:S(2)}, u32[]{:S(2)}) async-start(bf16[8,240,256]{2,1,0:T(8,128)(2,1)} %get-tuple-element.30), calls=%async_computation.2 | async-start | bytes 1966080 | tf_op jit(solution)/shard_map/all_to_all | solution.py:411
  131.6 0.9 copy-start.1
  142.2 20.1 %all-to-all-start.3 = ((bf16[16,224,128]{2,1,0:T(8,128)(2,1)}), bf16[16,224,128]{2,1,0:T(8,128)(2,1)S(1)}, u32[]{:S(2)}, u32[]{:S(2)}) async-start(bf16[16,224,128]{2,1,0:T(8,128)(2,1)} %shard_map.95), calls=%async_computation.3 | async-start | bytes 1835008 | tf_op jit(solution)/shard_map/all_to_all | solution.py:425
  163.4 17.8 %all-to-all-start.4 = ((bf16[16,224,128]{2,1,0:T(8,128)(2,1)}), bf16[16,224,128]{2,1,0:T(8,128)(2,1)S(1)}, u32[]{:S(2)}, u32[]{:S(2)}) async-start(bf16[16,224,128]{2,1,0:T(8,128)(2,1)} %shard_map.96), calls=%async_computation.4 | async-start | bytes 1835008 | tf_op jit(solution)/shard_map/all_to_all | solution.py:431
Sparse Core Ops, SparseCore 0:
  9.7 46.6 all-gather.3
  77.4 42.4 all-gather.5

commit v3 on v2

--- a/solution.py
+++ b/solution.py
@@ -28,8 +28,12 @@
 
 
 class Taps:
-    def __init__(self, ref):
-        self.ref = ref
+    def __init__(self, ref, coming=None):
+        self.ref, self.coming = ref, coming or {}
+
+    def arrive(self, gate, a):
+        if (gate, a) in self.coming:
+            self.coming.pop((gate, a)).wait()
 
     def rows(self, gate, tap):
         block = self.ref[:, gate * 9 + tap]
@@ -56,6 +60,8 @@
     total = None
     for a in range(3):
         lhs = xc[pl.ds(start + (a - 1) * PITCH, count), :]
+        for g in gates:
+            w.arrive(g, a)
         rhs = [jnp.concatenate([w.rows(g, 3 * a + b) for b in range(3)], axis=1) for g in gates]
         rhs = jnp.concatenate(rhs, axis=0) if len(rhs) > 1 else rhs[0]
         term = lax.dot_general(lhs, rhs, (((1,), (1,)), ((), ())), preferred_element_type=F32)
@@ -65,11 +71,22 @@
 
 def forward_kernel(
     above, middle, below, lab, ro, kernels,
-    u1, q1, c1, s1, u0, q0, c0, s0, s2, v, tot, w4, xc, ub, qb, sb, sem
+    u1, q1, c1, s1, u0, q0, c0, wst, s0, s2, v, tot, w4, xc, ubs, qbs, cbs, sb, sems
 ):
-    copy = pltpu.make_async_copy(kernels, w4, sem)
-    copy.start()
-    w = Taps(w4)
+    coming = {}
+    for a in range(3):
+        for g in range(2):
+            coming[g, a] = (kernels.at[:, pl.ds(g * 9 + 3 * a, 3)], w4.at[:, pl.ds(g * 9 + 3 * a, 3)])
+    coming[2, 0] = (kernels.at[:, 18:27], w4.at[:, 18:27])
+    for n, (key, (src, dst)) in enumerate(coming.items()):
+        coming[key] = pltpu.make_async_copy(src, dst, sems.at[8 + n])
+        coming[key].start()
+    w = Taps(w4, coming)
+    leaving = []
+
+    def leave(src, dst):
+        leaving.append(pltpu.make_async_copy(src, dst, sems.at[len(leaving)]))
+        leaving[-1].start()
 
     def window(k):
         parts = [ref[k * 8 * PITCH : (k + 1) * 8 * PITCH].astype(F32) for ref in (above, middle, below)]
@@ -85,6 +102,8 @@
             v[at : at + OWN_COLS] = ref[line : line + PITCH].astype(F32)[RIM : RIM + OWN_COLS].astype(BF)
     sb[...] = window(2)
     for step in range(2):
+        ub, qb, cb = ubs.at[step], qbs.at[step], cbs.at[step]
+        keep = pl.ds(6 * PITCH, 12 * PITCH) if step == 0 else pl.ds(4 * PITCH, 16 * PITCH)
         first = 1 + 2 * step
         count = (ROWS_IN - 2 * first) * PITCH
         start = first * PITCH
@@ -92,13 +111,13 @@
         put(xc, 0, PIX, C, 2 * C, True, sb[...])
         piece = count // CUTS
         v[2 * step * V_ROWS : (2 * step + 1) * V_ROWS] = halo_block(sb[7 * PITCH : 17 * PITCH])
-        if step == 0:
-            copy.wait()
         for i in range(CUTS):
             at = start + i * piece
             both = sigmoid(conv(xc, w, (0, 1), at, piece))
             ub[at : at + piece] = both[:, :C]
             qb[at : at + piece] = both[:, C:]
+        leave(ub.at[keep], (u0, u1)[step])
+        leave(qb.at[keep], (q0, q1)[step])
         rs = (qb[start : start + count] * sb[start : start + count]).astype(BF).astype(F32)
         v[(2 * step + 1) * V_ROWS : (2 * step + 2) * V_ROWS] = halo_block(rs[(7 - first) * PITCH : (17 - first) * PITCH])
         put(xc, start, count, C, 2 * C, True, rs)
@@ -112,22 +131,14 @@
             s = sb[at : at + piece]
             nxt = (1.0 - u) * s + u * cand
             nxt = jnp.where(wide(lab[at : at + piece]) > 0, nxt, 0.0).astype(BF).astype(F32)
-            if step == 0:
-                lo, hi = max(at, 6 * PITCH), min(at + piece, 18 * PITCH)
-                if lo < hi:
-                    c0[lo - 6 * PITCH : hi - 6 * PITCH] = cand[lo - at : hi - at]
-            else:
-                c1[at - 4 * PITCH : at - 4 * PITCH + piece] = cand
+            cb[at : at + piece] = cand
+            if step == 1:
                 s1[at - 4 * PITCH : at - 4 * PITCH + piece] = s.astype(BF)
-            qb_at = at
-            sb[qb_at : qb_at + piece] = nxt
+            sb[at : at + piece] = nxt
+        leave(cb.at[keep], (c0, c1)[step])
         if step == 0:
-            s0[...] = window(2)[6 * PITCH : 18 * PITCH].astype(BF)
-            u0[...] = ub[6 * PITCH : 18 * PITCH]
-            q0[...] = qb[6 * PITCH : 18 * PITCH]
-        else:
-            u1[...] = ub[4 * PITCH : 20 * PITCH]
-            q1[...] = qb[4 * PITCH : 20 * PITCH]
+            leave(w4.at[:, :, :, C:], wst)
+    s0[...] = window(2)[6 * PITCH : 18 * PITCH].astype(BF)
     last = sb[8 * PITCH : 16 * PITCH]
     s2[...] = last.astype(BF)
     rain = jnp.sum(last * ro[...], axis=1, keepdims=True)
@@ -141,6 +152,8 @@
         totals.append(jnp.sum(jnp.where(hit, rain, 0.0), axis=0, keepdims=True))
         counts.append(jnp.sum(jnp.where(hit, 1.0, 0.0), axis=0, keepdims=True))
     tot[...] = jnp.broadcast_to(jnp.concatenate(totals + counts, axis=0)[None], tot.shape)
+    for sent in leaving:
+        sent.wait()
 
 
 def adjoint(px, w, gates, start, count):
@@ -157,10 +170,21 @@
 
 
 def backward_kernel(
-    tp, tgt, lab, ro, u1, q1, c1, s1, u0, q0, c0, s0, s2, kernels, msg, loss, w4, px, gs, sem
+    tp, tgt, lab, ro, s1, s0, s2, hu1, hq1, hc1, hu0, hq0, hc0, kernels, msg, loss,
+    w4, px, gs, u1, q1, c1, u0, q0, c0, sems
 ):
-    copy = pltpu.make_async_copy(kernels.at[:, :, :, C:], w4, sem)
-    copy.start()
+    pairs = [
+        (hu1, u1), (hc1, c1), (kernels.at[:, 18:27], w4.at[:, 18:27]), (hq1, q1),
+        (kernels.at[:, 0:18], w4.at[:, 0:18]), (hu0, u0), (hc0, c0), (hq0, q0),
+    ]
+    coming = [pltpu.make_async_copy(src, dst, sems.at[n]) for n, (src, dst) in enumerate(pairs)]
+    for copy in coming:
+        copy.start()
+
+    def need(count):
+        for _ in range(count):
+            coming.pop(0).wait()
+
     w = Taps(w4)
     sums = jnp.sum(tp[...], axis=0)
     scale = 1.0 / (sums[4:8] + 1.0)
@@ -206,6 +230,7 @@
             return ref[(lo - first) * PITCH : (hi - first) * PITCH]
 
         lo, hi = first, first + rows
+        need(2)
         g = gs[lo * PITCH : hi * PITCH]
         cand = cv[...]
         pc = (g * uv[...] * (1.0 - cand * cand)).astype(BF).astype(F32)
@@ -213,8 +238,7 @@
         send(step * 3 + 2, pc[(8 - lo) * PITCH : (16 - lo) * PITCH])
         lo, hi = lo + 1, hi - 1
         n = (hi - lo) * PITCH
-        if step == 1:
-            copy.wait()
+        need(2 if step == 1 else 1)
         grs = adjoint(px, w, (2,), lo * PITCH, n)
         s = state(lo, hi)
         g = gs[lo * PITCH : hi * PITCH]
@@ -228,6 +252,7 @@
         send(step * 3 + 1, pq[(8 - lo) * PITCH : (16 - lo) * PITCH])
         lo, hi = lo + 1, hi - 1
         n = (hi - lo) * PITCH
+        need(1 if step == 1 else 0)
         g = gs[lo * PITCH : hi * PITCH] + adjoint(px, w, (0, 1), lo * PITCH, n)
         g = jnp.where(wide(lab[lo * PITCH : hi * PITCH]) > 0, g, 0.0)
         if step == 1:
@@ -236,14 +261,7 @@
             send(6, g)
 
 
-def corr_kernel(r, frames, gathered, out, vs, vf, p3, sems):
-    copies = [
-        pltpu.make_async_copy(frames, vf, sems.at[0]),
-        pltpu.make_async_copy(gathered, vs, sems.at[1]),
-    ]
-    for copy in copies:
-        copy.start()
-
+def corr_kernel(r, vf, vs, out, p3):
     def lanes_of(j, t):
         return r[j, t * 96 : t * 96 + 96, :].astype(F32)
 
@@ -264,9 +282,6 @@
                         g * 32 : g * 32 + 32
                     ].astype(BF)
 
-    for copy in copies:
-        copy.wait()
-
     def store(g, a, value, half):
         for b in range(3):
             slot = g * 9 + 3 * a + b
@@ -335,12 +350,12 @@
 HB = pl.BlockSpec(memory_space=pl.ANY)
 
 
-def call(kernel, specs, outs, scratch, flops, moved, *args, limit=VMEM_LIMIT):
+def call(kernel, specs, outs, scratch, flops, moved, *args, limit=VMEM_LIMIT, out_specs=None):
     return pl.pallas_call(
         kernel,
         out_shape=outs,
         in_specs=specs,
-        out_specs=jax.tree.map(lambda _: VM, outs),
+        out_specs=jax.tree.map(lambda _: VM, outs) if out_specs is None else out_specs,
         scratch_shapes=scratch,
         compiler_params=pltpu.CompilerParams(vmem_limit_bytes=limit),
         cost_estimate=pl.CostEstimate(flops=flops, bytes_accessed=moved, transcendentals=0),
@@ -385,42 +400,43 @@
     labels = jnp.broadcast_to(labels, (PIX, 128))
 
     n1, n0 = 16 * PITCH, 12 * PITCH
-    dma = pltpu.SemaphoreType.DMA(())
-    u1, q1, c1, s1, u0, q0, c0, s0, s2, v, tot = call(
+    u1, q1, c1, s1, u0, q0, c0, wst, s0, s2, v, tot = call(
         forward_kernel,
         [VM] * 5 + [HB],
         (
             shape(n1, C), shape(n1, C), shape(n1, C), shape(n1, C, dtype=BF),
-            shape(n0, C), shape(n0, C), shape(n0, C), shape(n0, C, dtype=BF), shape(8 * PITCH, C, dtype=BF),
+            shape(n0, C), shape(n0, C), shape(n0, C), shape(8, 27, 32, C, dtype=BF), shape(n0, C, dtype=BF), shape(8 * PITCH, C, dtype=BF),
             shape(V_ALL, C, dtype=BF), shape(128, 8, 128),
         ),
-        [pltpu.VMEM((8, 27, 32, 2 * C), BF), pltpu.VMEM((PIX, 6 * C), BF)] + [pltpu.VMEM((PIX, C), F32)] * 3 + [dma],
+        [pltpu.VMEM((8, 27, 32, 2 * C), BF), pltpu.VMEM((PIX, 6 * C), BF)]
+        + [pltpu.VMEM((2, PIX, C), F32)] * 3 + [pltpu.VMEM((PIX, C), F32), pltpu.SemaphoreType.DMA((15,))],
         13_000_000_000, 20_000_000,
         above, middle, below, labels, ro, kernels,
+        out_specs=(HB, HB, HB, VM, HB, HB, HB, HB) + (VM,) * 4,
     )
     tp = lax.all_to_all(tot, ("rows", "chan"), 0, 0)
     vs = lax.all_gather(v, "chan", axis=0)
     msg, loss = call(
         backward_kernel,
-        [VM] * 13 + [HB],
+        [VM] * 7 + [HB] * 7,
         (shape(8, 240, C, dtype=BF), shape(8, 128)),
-        [pltpu.VMEM((8, 27, 32, C), BF), pltpu.VMEM((PIX, 6 * C), BF), pltpu.VMEM((PIX, C), F32), dma],
+        [pltpu.VMEM((8, 27, 32, C), BF), pltpu.VMEM((PIX, 6 * C), BF), pltpu.VMEM((PIX, C), F32)]
+        + [pltpu.VMEM((n, C), F32) for n in (n1, n1, n1, n0, n0, n0)] + [pltpu.SemaphoreType.DMA((8,))],
         4_000_000_000, 20_000_000,
-        tp, targets.reshape(4, 128), labels, ro, u1, q1, c1, s1, u0, q0, c0, s0, s2, kernels,
+        tp, targets.reshape(4, 128), labels, ro, s1, s0, s2,
+        u1, q1, c1, u0, q0, c0, wst,
     )
     got = lax.all_to_all(msg, "chan", 0, 0)
     hidden_grad = got[:, 192:224].reshape(8, 32, 8, OWN_COLS)
     hidden_grad = jnp.transpose(hidden_grad, (1, 2, 0, 3)).reshape(32, 8, 8 * OWN_COLS).astype(F32)
     part = call(
         corr_kernel,
-        [VM, HB, HB],
+        [VM] * 3,
         shape(16, 224, 128, dtype=BF),
-        [
-            pltpu.VMEM((8, V_ALL, C), BF), pltpu.VMEM((2, 8, 8, OWN_COLS, C), BF),
-            pltpu.VMEM((288, 16 * OWN), BF), pltpu.SemaphoreType.DMA((2,)),
-        ],
+        [pltpu.VMEM((288, 16 * OWN), BF)],
         4_000_000_000, 10_000_000,
         got, turned.reshape(2, 8, 8, OWN_COLS, C), vs,
+        limit=24 * 1024 * 1024,
     )
     mine = lax.all_to_all(part, "rows", 0, 0)
     last = (row_tile % 4 == 3).astype(jnp.int32)[None]

time: 191 us -> 188 us (0.984)
  Pallas kernels: 45 us -> 39.1 us
  local copies, waits for them, and re-layouts: 15.3 us -> 18.1 us
    ppermute x1, waiting for transfers between devices: 8.75 us -> 1.15 us  [per_device(): above = lax.ppermute(middle, 'rows', up)]
    ppermute x1, waiting for transfers between devices: 4.32 us -> 10.2 us  [per_device(): below = lax.ppermute(middle, 'rows', down)]
    pallas_call x5, Pallas kernels: 45 us -> 39.1 us  [call(): pl.pallas_call(kernel, out_shape=outs, in_specs=specs, out_specs=jax.tree...]
    all_gather x1, waiting for transfers between devices: 10.1 us -> 14.9 us  [per_device(): kernels = lax.all_gather(own_kernel, 'chan', axis=0)]
    unnamed x17 -> x23, local copies, waits for them, and re-layouts: 1.03 us -> 3.65 us
    convert_element_type x3, local copies, waits for them, and re-layouts: 1.89 us -> 4.09 us  [per_device(): jnp.transpose(hidden_grad, (1, 2, 0, 3)).reshape(32, 8, 8 * OWN_COLS)]
  transfers between devices with their start and end apart: 8 -> 8, of which waited for: 7 -> 7; matrix products, arithmetic and copies ran while one was open for 8% -> 7% of each run, Pallas kernels for 7% -> 7%
where the time goes in v3:
time: 188 us; the launch traced here: 187 us
  waiting for transfers between devices  70.1 us (37%)
  Pallas kernels  39.1 us (21%)
  starting transfers between devices  22.5 us (12%)
  blocking collectives  22.5 us (12%)
  local copies, waits for them, and re-layouts  18.1 us (10%)
  between operations  14.3 us (8%)
    pallas_call x5, Pallas kernels, call(): pl.pallas_call(kernel, out_shape=outs, in_specs=specs, out_specs=jax.tree...  39.1 us
    all_to_all x1, blocking collectives, per_device(): tp = lax.all_to_all(tot, ('rows', 'chan'), 0, 0)  22.5 us
    all_to_all x1, waiting for transfers between devices, per_device(): mine = lax.all_to_all(part, 'rows', 0, 0)  16.2 us
    all_gather x1, waiting for transfers between devices, per_device(): kernels = lax.all_gather(own_kernel, 'chan', axis=0)  14.9 us
    all_to_all x1, waiting for transfers between devices, per_device(): got = lax.all_to_all(msg, 'chan', 0, 0)  12.2 us
    ppermute x1, waiting for transfers between devices, per_device(): below = lax.ppermute(middle, 'rows', down)  10.2 us
    all_to_all x1, waiting for transfers between devices, per_device(): whole = lax.all_to_all(mine, 'rows', 0, 0)  8.85 us
    all_to_all x1, waiting for transfers between devices, per_device(): pieces = lax.all_to_all(pieces, 'chan', 0, 0)  5.95 us
  transfers between devices with their start and end apart: 8, of which 7 were waited for; matrix products, arithmetic and copies ran while one was open for 7% of the time, Pallas kernels for 7%

profile of v3, /device:TPU:0, one launch (start us, length us, event | category | flops | bytes accessed | tf_op | source)
XLA Modules:
  0.0 187.4 jit_solution(3624044513162768909)
XLA Ops:
  7.2 0.0 copy-start.5
  7.2 0.0 all-gather.4.cloned.1.call-start
  7.2 0.7 all-gather.4.cloned.1.call-update
  7.9 0.0 copy-start.4
  7.9 0.0 copy-start.2
  7.9 1.5 pad_slice_fusion
  9.4 0.1 stack.44
  9.5 0.1 stack.41
  9.6 0.1 stack.40
  9.7 0.1 stack.39
  9.8 0.1 stack.38
  10.0 0.1 stack.37
  10.1 0.1 stack.43
  10.2 0.1 stack.42
  10.3 0.0 copy-done.5
  10.4 0.7 pad_maximum_fusion
  11.2 4.6 %all-to-all-start = ((bf16[8,33,384]{2,1,0:T(8,128)(2,1)}), bf16[8,33,384]{2,1,0:T(8,128)(2,1)S(1)}, u32[]{:S(2)}, u32[]{:S(2)}) async-start(bf16[8,33,384]{2,1,0:T(8,128)(2,1)} %pad_maximum_fusion), calls=%async_computation | async-start | bytes 491520 | tf_op jit(solution)/shard_map/all_to_all | solution.py:387
  15.7 0.0 all-gather.6.cloned.1.call-start
  15.8 0.0 copy-done.4
  15.8 0.1 pad_dynamic-slice_fusion.1
  15.9 0.1 reshape.102
  16.0 0.0 copy-done.2
  16.0 0.5 pad_dynamic-slice_fusion
  16.5 0.6 copy.26
  17.1 5.9 %all-to-all-done = bf16[8,33,384]{2,1,0:T(8,128)(2,1)S(1)} async-done(((bf16[8,33,384]{2,1,0:T(8,128)(2,1)}), bf16[8,33,384]{2,1,0:T(8,128)(2,1)S(1)}, u32[]{:S(2)}, u32[]{:S(2)}) %all-to-all-start) | async-done | bytes 202784 | tf_op jit(solution)/shard_map/all_to_all | solution.py:387
  23.1 0.1 copy.27
  23.3 0.0 copy-start.3
  23.3 1.3 collective-permute-start.1
  24.6 4.8 %collective-permute-start = (bf16[1168,256]{1,0:T(8,128)(2,1)S(1)}, bf16[1168,256]{1,0:T(8,128)(2,1)S(1)}, u32[]{:S(2)}, u32[]{:S(2)}) collective-permute-start(bf16[1168,256]{1,0:T(8,128)(2,1)S(1)} %fusion.1.middle), channel_id=1, source_target_pairs={{0,8},{8,16},{16,24},{24,32},{32,40},{40,48},{48,56},{56,64},{64,7... | collective-permute-start | bytes 1794056 | tf_op jit(solution)/shard_map/ppermute | solution.py:395
  29.4 0.7 reshape.106.ro
  30.1 10.2 %collective-permute-done.1.below = bf16[1168,256]{1,0:T(8,128)(2,1)S(1)} collective-permute-done((bf16[1168,256]{1,0:T(8,128)(2,1)S(1)}, bf16[1168,256]{1,0:T(8,128)(2,1)S(1)}, u32[]{:S(2)}, u32[]{:S(2)}) %collective-permute-start.1) | collective-permute-done | bytes 598048 | tf_op jit(solution)/shard_map/ppermute | solution.py:396
  40.3 0.0 copy-start.6
  40.3 1.2 collective-permute-done.above
  41.5 0.0 copy-start.7
  41.6 14.9 %all-gather.4.cloned.1.call-done.kernels = bf16[8,27,32,512]{3,2,1,0:T(8,128)(2,1)} async-done(((bf16[1,27,32,512]{3,2,1,0:T(8,128)(2,1)}), bf16[8,27,32,512]{3,2,1,0:T(8,128)(2,1)}) %all-gather.4.cloned.1.call-update) | async-done | bytes 7077904 | tf_op jit(solution)/shard_map/all_gather | solution.py:386
  56.4 1.0 broadcast_in_dim.14.lab
  57.5 0.0 copy-done.3
  57.5 0.0 copy-done.6
  57.5 0.0 copy-done.7
  57.5 19.9 %shard_map.93 = (f32[768,256]{1,0:T(8,128)}, f32[768,256]{1,0:T(8,128)}, f32[768,256]{1,0:T(8,128)}, bf16[768,256]{1,0:T(8,128)(2,1)}, f32[576,256]{1,0:T(8,128)...) custom-call(bf16[1168,256]{1,0:T(8,128)(2,1)} %copy-done.7, ...), custom_call_target="tpu_custom_call" | custom-call | flops 12999999488 | bytes 20000000 | tf_op jit(solution)/shard_map/pallas_call | solution.py:354
  77.4 0.0 all-gather.6.cloned.1.call-update
  77.4 22.5 %all_to_all.25.tp = f32[128,8,128]{2,1,0:T(8,128)} all-to-all(f32[128,8,128]{2,1,0:T(8,128)} %get-tuple-element.20), channel_id=1, replica_groups=mesh['rows'=16,'chan'=8] {'rows','chan'}, dimensions={0} | all-to-all | bytes 1048576 | tf_op jit(solution)/shard_map/all_to_all | solution.py:417
  99.9 12.4 %shard_map.94 = (bf16[8,240,256]{2,1,0:T(8,128)(2,1)}, f32[8,128]{1,0:T(8,128)}) custom-call(f32[128,8,128]{2,1,0:T(8,128)} %all_to_all.25.tp, f32[4,128]{1,0:T(4,128)} %bitcast.30, s32[1152,128]{1,0:T(8,128)} %broadcast_in_dim.14.lab, f32[1,256]{1,0:T(1,128)} %reshape.106.ro, bf16[768,256]{1,0:T(8,128)(2,1)} %get-tuple-element.21.s1, ...), custom_call_target="tpu_custom_call" | custom-call | flops 4000000000 | bytes 20000000 | tf_op jit(solution)/shard_map/pallas_call | solution.py:354
  112.3 3.6 %all-to-all-start.2 = ((bf16[8,240,256]{2,1,0:T(8,128)(2,1)}), bf16[8,240,256]{2,1,0:T(8,128)(2,1)S(1)}, u32[]{:S(2)}, u32[]{:S(2)}) async-start(bf16[8,240,256]{2,1,0:T(8,128)(2,1)} %get-tuple-element.32), calls=%async_computation.2 | async-start | bytes 1966080 | tf_op jit(solution)/shard_map/all_to_all | solution.py:429
  115.9 3.0 %copy.28 = bf16[2,8,256,256]{3,2,1,0:T(8,128)(2,1)S(1)} copy(bf16[2,8,256,256]{2,1,3,0:T(8,128)(2,1)} %bitcast.22) | data formatting | bytes 4194304 | tf_op jit(solution)/shard_map/transpose | solution.py:388
  118.9 12.2 %all-to-all-done.2.r = bf16[8,240,256]{2,1,0:T(8,128)(2,1)S(1)} async-done(((bf16[8,240,256]{2,1,0:T(8,128)(2,1)}), bf16[8,240,256]{2,1,0:T(8,128)(2,1)S(1)}, u32[]{:S(2)}, u32[]{:S(2)}) %all-to-all-start.2) | async-done | bytes 983072 | tf_op jit(solution)/shard_map/all_to_all | solution.py:429
  131.1 0.0 all-gather.6.cloned.1.call-done
  131.1 0.0 copy-start.1
  131.1 2.6 %copy-done.1 = bf16[11264,256]{1,0:T(8,128)(2,1)S(1)} copy-done((bf16[11264,256]{1,0:T(8,128)(2,1)S(1)}, bf16[11264,256]{1,0:T(8,128)(2,1)}, u32[]{:S(2)}) %copy-start.1) | copy-done | bytes 5767192
  133.7 4.2 %shard_map.95 = bf16[16,224,128]{2,1,0:T(8,128)(2,1)S(1)} custom-call(bf16[8,240,256]{2,1,0:T(8,128)(2,1)S(1)} %all-to-all-done.2.r, bf16[2,8,8,32,256]{4,3,2,1,0:T(8,128)(2,1)S(1)} %bitcast.20, bf16[8,1408,256]{2,1,0:T(8,128)(2,1)S(1)} %bitcast.21), custom_call_target="tpu_custom_call" | custom-call | flops 4000000000 | bytes 10000000 | tf_op jit(solution)/shard_map/pallas_call | solution.py:354
  138.0 0.0 copy-start
  138.0 0.9 copy-done
  138.9 4.6 %all-to-all-start.3 = ((bf16[16,224,128]{2,1,0:T(8,128)(2,1)}), bf16[16,224,128]{2,1,0:T(8,128)(2,1)S(1)}, u32[]{:S(2)}, u32[]{:S(2)}) async-start(bf16[16,224,128]{2,1,0:T(8,128)(2,1)} %copy-done), calls=%async_computation.3 | async-start | bytes 1835008 | tf_op jit(solution)/shard_map/all_to_all | solution.py:441
  143.5 16.2 %all-to-all-done.3.parts = bf16[16,224,128]{2,1,0:T(8,128)(2,1)S(1)} async-done(((bf16[16,224,128]{2,1,0:T(8,128)(2,1)}), bf16[16,224,128]{2,1,0:T(8,128)(2,1)S(1)}, u32[]{:S(2)}, u32[]{:S(2)}) %all-to-all-start.3) | async-done | bytes 917536 | tf_op jit(solution)/shard_map/all_to_all | solution.py:441
  159.7 1.1 shard_map.96
  160.8 3.6 %all-to-all-start.4 = ((bf16[16,224,128]{2,1,0:T(8,128)(2,1)}), bf16[16,224,128]{2,1,0:T(8,128)(2,1)S(1)}, u32[]{:S(2)}, u32[]{:S(2)}) async-start(bf16[16,224,128]{2,1,0:T(8,128)(2,1)} %shard_map.96), calls=%async_computation.4 | async-start | bytes 1835008 | tf_op jit(solution)/shard_map/all_to_all | solution.py:447
  164.4 1.2 slice.69
  165.6 0.3 reshape.109
  165.9 1.6 copy.29
  167.5 2.2 %reshape.108 = f32[32,8,256]{2,1,0:T(8,128)} reshape(f32[32,8,8,32]{3,2,1,0:T(8,128)} %copy.29) | data formatting | bytes 524288 | tf_op jit(solution)/shard_map/convert_element_type | solution.py:431
  169.7 8.8 %all-to-all-done.4.parts = bf16[16,224,128]{2,1,0:T(8,128)(2,1)S(1)} async-done(((bf16[16,224,128]{2,1,0:T(8,128)(2,1)}), bf16[16,224,128]{2,1,0:T(8,128)(2,1)S(1)}, u32[]{:S(2)}, u32[]{:S(2)}) %all-to-all-start.4) | async-done | bytes 917536 | tf_op jit(solution)/shard_map/all_to_all | solution.py:447
  178.6 1.4 shard_map.97
  180.0 0.6 fusion.5
  (26 shorter events, 0.4 us)
Async XLA Ops:
  7.2 3.1 %copy-start.5 = (bf16[32]{0:T(256)(128)(2,1)S(1)}, bf16[32]{0:T(256)(128)(2,1)}, u32[]{:S(2)}) copy-start(bf16[32]{0:T(256)(128)(2,1)} %param.9) | copy-start | bytes 196
  7.2 49.3 %all-gather.4.cloned.1.call-start = ((), (), s32[]{:S(2)}) async-start(), calls=%async_computation.5 | async-start | bytes 7962624 | tf_op jit(solution)/shard_map/all_gather | solution.py:386
  7.9 7.9 %copy-start.4 = (s32[8,256]{1,0:T(8,128)S(1)}, s32[8,256]{1,0:T(8,128)}, u32[]{:S(2)}) copy-start(s32[8,256]{1,0:T(8,128)} %param.10) | copy-start | bytes 24580
  7.9 8.1 %copy-start.2 = (bf16[2,256,8,256]{3,2,1,0:T(8,128)(2,1)S(1)}, bf16[2,256,8,256]{3,2,1,0:T(8,128)(2,1)}, u32[]{:S(2)}) copy-start(bf16[2,256,8,256]{3,2,1,0:T(8,128)(2,1)} %param.6) | copy-start | bytes 6291460
  11.2 11.9 %all-to-all-start = ((bf16[8,33,384]{2,1,0:T(8,128)(2,1)}), bf16[8,33,384]{2,1,0:T(8,128)(2,1)S(1)}, u32[]{:S(2)}, u32[]{:S(2)}) async-start(bf16[8,33,384]{2,1,0:T(8,128)(2,1)} %pad_maximum_fusion), calls=%async_computation | async-start | bytes 491520 | tf_op jit(solution)/shard_map/all_to_all | solution.py:387
  15.7 115.3 %all-gather.6.cloned.1.call-start = ((), (), s32[]{:S(2)}) async-start(), calls=%async_computation.6 | async-start | bytes 6488064 | tf_op jit(solution)/shard_map/all_gather | solution.py:418
  23.3 34.2 %copy-start.3 = (bf16[1168,256]{1,0:T(8,128)(2,1)}, bf16[1168,256]{1,0:T(8,128)(2,1)S(1)}, u32[]{:S(2)}) copy-start(bf16[1168,256]{1,0:T(8,128)(2,1)S(1)} %fusion.1.middle) | copy-start | bytes 1794052
  23.3 17.0 %collective-permute-start.1 = (bf16[1168,256]{1,0:T(8,128)(2,1)S(1)}, bf16[1168,256]{1,0:T(8,128)(2,1)S(1)}, u32[]{:S(2)}, u32[]{:S(2)}) collective-permute-start(bf16[1168,256]{1,0:T(8,128)(2,1)S(1)} %fusion.1.middle), channel_id=1, source_target_pairs={{8,0},{16,8},{24,16},{32,24},{40,32},{48,40},{56,48},{64,56},{72,6... | collective-permute-start | bytes 1794056 | tf_op jit(solution)/shard_map/ppermute | solution.py:396
  24.6 16.9 %collective-permute-start = (bf16[1168,256]{1,0:T(8,128)(2,1)S(1)}, bf16[1168,256]{1,0:T(8,128)(2,1)S(1)}, u32[]{:S(2)}, u32[]{:S(2)}) collective-permute-start(bf16[1168,256]{1,0:T(8,128)(2,1)S(1)} %fusion.1.middle), channel_id=1, source_target_pairs={{0,8},{8,16},{16,24},{24,32},{32,40},{40,48},{48,56},{56,64},{64,7... | collective-permute-start | bytes 1794056 | tf_op jit(solution)/shard_map/ppermute | solution.py:395
  40.3 17.2 %copy-start.6 = (bf16[1168,256]{1,0:T(8,128)(2,1)}, bf16[1168,256]{1,0:T(8,128)(2,1)S(1)}, u32[]{:S(2)}) copy-start(bf16[1168,256]{1,0:T(8,128)(2,1)S(1)} %collective-permute-done.1.below) | copy-start | bytes 1794052
  41.5 16.0 %copy-start.7 = (bf16[1168,256]{1,0:T(8,128)(2,1)}, bf16[1168,256]{1,0:T(8,128)(2,1)S(1)}, u32[]{:S(2)}) copy-start(bf16[1168,256]{1,0:T(8,128)(2,1)S(1)} %collective-permute-done.above) | copy-start | bytes 1794052
  112.3 18.8 %all-to-all-start.2 = ((bf16[8,240,256]{2,1,0:T(8,128)(2,1)}), bf16[8,240,256]{2,1,0:T(8,128)(2,1)S(1)}, u32[]{:S(2)}, u32[]{:S(2)}) async-start(bf16[8,240,256]{2,1,0:T(8,128)(2,1)} %get-tuple-element.32), calls=%async_computation.2 | async-start | bytes 1966080 | tf_op jit(solution)/shard_map/all_to_all | solution.py:429
  131.1 2.6 %copy-start.1 = (bf16[11264,256]{1,0:T(8,128)(2,1)S(1)}, bf16[11264,256]{1,0:T(8,128)(2,1)}, u32[]{:S(2)}) copy-start(bf16[11264,256]{1,0:T(8,128)(2,1)} %all-gather.6.cloned.1.call-done) | copy-start | bytes 17301508
  138.0 0.9 copy-start
  138.9 20.8 %all-to-all-start.3 = ((bf16[16,224,128]{2,1,0:T(8,128)(2,1)}), bf16[16,224,128]{2,1,0:T(8,128)(2,1)S(1)}, u32[]{:S(2)}, u32[]{:S(2)}) async-start(bf16[16,224,128]{2,1,0:T(8,128)(2,1)} %copy-done), calls=%async_computation.3 | async-start | bytes 1835008 | tf_op jit(solution)/shard_map/all_to_all | solution.py:441
  160.8 17.8 %all-to-all-start.4 = ((bf16[16,224,128]{2,1,0:T(8,128)(2,1)}), bf16[16,224,128]{2,1,0:T(8,128)(2,1)S(1)}, u32[]{:S(2)}, u32[]{:S(2)}) async-start(bf16[16,224,128]{2,1,0:T(8,128)(2,1)} %shard_map.96), calls=%async_computation.4 | async-start | bytes 1835008 | tf_op jit(solution)/shard_map/all_to_all | solution.py:447
Sparse Core Ops, SparseCore 0:
  9.7 46.6 all-gather.3
  77.5 42.5 all-gather.5

commit v4 on v3

--- a/solution.py
+++ b/solution.py
@@ -157,6 +157,11 @@
 
 
 def adjoint(px, w, gates, start, count):
+    half = count // 2
+    return jnp.concatenate([adjoint_rows(px, w, gates, at, half) for at in (start, start + half)], axis=0)
+
+
+def adjoint_rows(px, w, gates, start, count):
     total = None
     width = len(gates) * C
     for a in range(3):

time: 188 us -> 188 us (level)
  Pallas kernels: 39.1 us -> 36.4 us
  starting transfers between devices: 22.5 us -> 24.6 us
    pallas_call x5, Pallas kernels: 39.1 us -> 36.4 us  [call(): pl.pallas_call(kernel, out_shape=outs, in_specs=specs, out_specs=jax.tree...]
    all_to_all x1, starting transfers between devices: 4.59 us -> 6.72 us  [per_device(): mine = lax.all_to_all(part, 'rows', 0, 0)]
  transfers between devices with their start and end apart: 8 -> 8, of which waited for: 7 -> 7; matrix products, arithmetic and copies ran while one was open for 7% -> 7% of each run, Pallas kernels for 7% -> 5%
where the time goes in v4:
time: 188 us; the launch traced here: 187 us
  waiting for transfers between devices  70.7 us (38%)
  Pallas kernels  36.4 us (19%)
  starting transfers between devices  24.6 us (13%)
  blocking collectives  22.5 us (12%)
  local copies, waits for them, and re-layouts  18.1 us (10%)
  between operations  14.3 us (8%)
    pallas_call x5, Pallas kernels, call(): pl.pallas_call(kernel, out_shape=outs, in_specs=specs, out_specs=jax.tree...  36.4 us
    all_to_all x1, blocking collectives, per_device(): tp = lax.all_to_all(tot, ('rows', 'chan'), 0, 0)  22.5 us
    all_to_all x1, waiting for transfers between devices, per_device(): mine = lax.all_to_all(part, 'rows', 0, 0)  16.2 us
    all_gather x1, waiting for transfers between devices, per_device(): kernels = lax.all_gather(own_kernel, 'chan', axis=0)  14.9 us
    all_to_all x1, waiting for transfers between devices, per_device(): got = lax.all_to_all(msg, 'chan', 0, 0)  12.7 us
    ppermute x1, waiting for transfers between devices, per_device(): below = lax.ppermute(middle, 'rows', down)  10.2 us
    all_to_all x1, waiting for transfers between devices, per_device(): whole = lax.all_to_all(mine, 'rows', 0, 0)  8.85 us
    all_to_all x1, starting transfers between devices, per_device(): mine = lax.all_to_all(part, 'rows', 0, 0)  6.72 us
  transfers between devices with their start and end apart: 8, of which 7 were waited for; matrix products, arithmetic and copies ran while one was open for 7% of the time, Pallas kernels for 5%

profile of v4, /device:TPU:0, one launch (start us, length us, event | category | flops | bytes accessed | tf_op | source)
XLA Modules:
  0.0 187.4 jit_solution(2728839642963435649)
XLA Ops:
  7.2 0.0 copy-start.5
  7.2 0.0 all-gather.4.cloned.1.call-start
  7.2 0.7 all-gather.4.cloned.1.call-update
  7.9 0.0 copy-start.4
  7.9 0.0 copy-start.2
  7.9 1.5 pad_slice_fusion
  9.4 0.1 stack.44
  9.5 0.1 stack.41
  9.6 0.1 stack.40
  9.7 0.1 stack.39
  9.8 0.1 stack.38
  10.0 0.1 stack.37
  10.1 0.1 stack.43
  10.2 0.1 stack.42
  10.3 0.0 copy-done.5
  10.4 0.7 pad_maximum_fusion
  11.2 4.6 %all-to-all-start = ((bf16[8,33,384]{2,1,0:T(8,128)(2,1)}), bf16[8,33,384]{2,1,0:T(8,128)(2,1)S(1)}, u32[]{:S(2)}, u32[]{:S(2)}) async-start(bf16[8,33,384]{2,1,0:T(8,128)(2,1)} %pad_maximum_fusion), calls=%async_computation | async-start | bytes 491520 | tf_op jit(solution)/shard_map/all_to_all | solution.py:392
  15.7 0.0 all-gather.6.cloned.1.call-start
  15.8 0.0 copy-done.4
  15.8 0.1 pad_dynamic-slice_fusion.1
  15.9 0.1 reshape.102
  16.0 0.0 copy-done.2
  16.0 0.5 pad_dynamic-slice_fusion
  16.5 0.6 copy.26
  17.1 5.9 %all-to-all-done = bf16[8,33,384]{2,1,0:T(8,128)(2,1)S(1)} async-done(((bf16[8,33,384]{2,1,0:T(8,128)(2,1)}), bf16[8,33,384]{2,1,0:T(8,128)(2,1)S(1)}, u32[]{:S(2)}, u32[]{:S(2)}) %all-to-all-start) | async-done | bytes 202784 | tf_op jit(solution)/shard_map/all_to_all | solution.py:392
  23.1 0.1 copy.27
  23.3 0.0 copy-start.3
  23.3 1.3 collective-permute-start.1
  24.6 4.8 %collective-permute-start = (bf16[1168,256]{1,0:T(8,128)(2,1)S(1)}, bf16[1168,256]{1,0:T(8,128)(2,1)S(1)}, u32[]{:S(2)}, u32[]{:S(2)}) collective-permute-start(bf16[1168,256]{1,0:T(8,128)(2,1)S(1)} %fusion.1.middle), channel_id=1, source_target_pairs={{0,8},{8,16},{16,24},{24,32},{32,40},{40,48},{48,56},{56,64},{64,7... | collective-permute-start | bytes 1794056 | tf_op jit(solution)/shard_map/ppermute | solution.py:400
  29.4 0.7 reshape.106.ro
  30.1 10.2 %collective-permute-done.1.below = bf16[1168,256]{1,0:T(8,128)(2,1)S(1)} collective-permute-done((bf16[1168,256]{1,0:T(8,128)(2,1)S(1)}, bf16[1168,256]{1,0:T(8,128)(2,1)S(1)}, u32[]{:S(2)}, u32[]{:S(2)}) %collective-permute-start.1) | collective-permute-done | bytes 598048 | tf_op jit(solution)/shard_map/ppermute | solution.py:401
  40.3 0.0 copy-start.6
  40.3 1.2 collective-permute-done.above
  41.5 0.0 copy-start.7
  41.6 14.9 %all-gather.4.cloned.1.call-done.kernels = bf16[8,27,32,512]{3,2,1,0:T(8,128)(2,1)} async-done(((bf16[1,27,32,512]{3,2,1,0:T(8,128)(2,1)}), bf16[8,27,32,512]{3,2,1,0:T(8,128)(2,1)}) %all-gather.4.cloned.1.call-update) | async-done | bytes 7077904 | tf_op jit(solution)/shard_map/all_gather | solution.py:391
  56.4 1.0 broadcast_in_dim.14.lab
  57.5 0.0 copy-done.3
  57.5 0.0 copy-done.6
  57.5 0.0 copy-done.7
  57.5 19.9 %shard_map.93 = (f32[768,256]{1,0:T(8,128)}, f32[768,256]{1,0:T(8,128)}, f32[768,256]{1,0:T(8,128)}, bf16[768,256]{1,0:T(8,128)(2,1)}, f32[576,256]{1,0:T(8,128)...) custom-call(bf16[1168,256]{1,0:T(8,128)(2,1)} %copy-done.7, ...), custom_call_target="tpu_custom_call" | custom-call | flops 12999999488 | bytes 20000000 | tf_op jit(solution)/shard_map/pallas_call | solution.py:359
  77.4 0.0 all-gather.6.cloned.1.call-update
  77.4 22.5 %all_to_all.25.tp = f32[128,8,128]{2,1,0:T(8,128)} all-to-all(f32[128,8,128]{2,1,0:T(8,128)} %get-tuple-element.20), channel_id=1, replica_groups=mesh['rows'=16,'chan'=8] {'rows','chan'}, dimensions={0} | all-to-all | bytes 1048576 | tf_op jit(solution)/shard_map/all_to_all | solution.py:422
  99.9 9.7 %shard_map.94 = (bf16[8,240,256]{2,1,0:T(8,128)(2,1)}, f32[8,128]{1,0:T(8,128)}) custom-call(f32[128,8,128]{2,1,0:T(8,128)} %all_to_all.25.tp, f32[4,128]{1,0:T(4,128)} %bitcast.30, s32[1152,128]{1,0:T(8,128)} %broadcast_in_dim.14.lab, f32[1,256]{1,0:T(1,128)} %reshape.106.ro, bf16[768,256]{1,0:T(8,128)(2,1)} %get-tuple-element.21.s1, ...), custom_call_target="tpu_custom_call" | custom-call | flops 4000000000 | bytes 20000000 | tf_op jit(solution)/shard_map/pallas_call | solution.py:359
  109.6 3.6 %all-to-all-start.2 = ((bf16[8,240,256]{2,1,0:T(8,128)(2,1)}), bf16[8,240,256]{2,1,0:T(8,128)(2,1)S(1)}, u32[]{:S(2)}, u32[]{:S(2)}) async-start(bf16[8,240,256]{2,1,0:T(8,128)(2,1)} %get-tuple-element.32), calls=%async_computation.2 | async-start | bytes 1966080 | tf_op jit(solution)/shard_map/all_to_all | solution.py:434
  113.2 3.0 %copy.28 = bf16[2,8,256,256]{3,2,1,0:T(8,128)(2,1)S(1)} copy(bf16[2,8,256,256]{2,1,3,0:T(8,128)(2,1)} %bitcast.22) | data formatting | bytes 4194304 | tf_op jit(solution)/shard_map/transpose | solution.py:393
  116.2 12.7 %all-to-all-done.2.r = bf16[8,240,256]{2,1,0:T(8,128)(2,1)S(1)} async-done(((bf16[8,240,256]{2,1,0:T(8,128)(2,1)}), bf16[8,240,256]{2,1,0:T(8,128)(2,1)S(1)}, u32[]{:S(2)}, u32[]{:S(2)}) %all-to-all-start.2) | async-done | bytes 983072 | tf_op jit(solution)/shard_map/all_to_all | solution.py:434
  128.9 0.0 all-gather.6.cloned.1.call-done
  128.9 0.0 copy-start.1
  128.9 2.6 %copy-done.1 = bf16[11264,256]{1,0:T(8,128)(2,1)S(1)} copy-done((bf16[11264,256]{1,0:T(8,128)(2,1)S(1)}, bf16[11264,256]{1,0:T(8,128)(2,1)}, u32[]{:S(2)}) %copy-start.1) | copy-done | bytes 5767192
  131.6 4.2 %shard_map.95 = bf16[16,224,128]{2,1,0:T(8,128)(2,1)S(1)} custom-call(bf16[8,240,256]{2,1,0:T(8,128)(2,1)S(1)} %all-to-all-done.2.r, bf16[2,8,8,32,256]{4,3,2,1,0:T(8,128)(2,1)S(1)} %bitcast.20, bf16[8,1408,256]{2,1,0:T(8,128)(2,1)S(1)} %bitcast.21), custom_call_target="tpu_custom_call" | custom-call | flops 4000000000 | bytes 10000000 | tf_op jit(solution)/shard_map/pallas_call | solution.py:359
  135.8 0.0 copy-start
  135.8 0.9 copy-done
  136.8 6.7 %all-to-all-start.3 = ((bf16[16,224,128]{2,1,0:T(8,128)(2,1)}), bf16[16,224,128]{2,1,0:T(8,128)(2,1)S(1)}, u32[]{:S(2)}, u32[]{:S(2)}) async-start(bf16[16,224,128]{2,1,0:T(8,128)(2,1)} %copy-done), calls=%async_computation.3 | async-start | bytes 1835008 | tf_op jit(solution)/shard_map/all_to_all | solution.py:446
  143.5 16.2 %all-to-all-done.3.parts = bf16[16,224,128]{2,1,0:T(8,128)(2,1)S(1)} async-done(((bf16[16,224,128]{2,1,0:T(8,128)(2,1)}), bf16[16,224,128]{2,1,0:T(8,128)(2,1)S(1)}, u32[]{:S(2)}, u32[]{:S(2)}) %all-to-all-start.3) | async-done | bytes 917536 | tf_op jit(solution)/shard_map/all_to_all | solution.py:446
  159.7 1.1 shard_map.96
  160.8 3.6 %all-to-all-start.4 = ((bf16[16,224,128]{2,1,0:T(8,128)(2,1)}), bf16[16,224,128]{2,1,0:T(8,128)(2,1)S(1)}, u32[]{:S(2)}, u32[]{:S(2)}) async-start(bf16[16,224,128]{2,1,0:T(8,128)(2,1)} %shard_map.96), calls=%async_computation.4 | async-start | bytes 1835008 | tf_op jit(solution)/shard_map/all_to_all | solution.py:452
  164.4 1.2 slice.69
  165.6 0.3 reshape.109
  165.9 1.6 copy.29
  167.5 2.2 %reshape.108 = f32[32,8,256]{2,1,0:T(8,128)} reshape(f32[32,8,8,32]{3,2,1,0:T(8,128)} %copy.29) | data formatting | bytes 524288 | tf_op jit(solution)/shard_map/convert_element_type | solution.py:436
  169.7 8.8 %all-to-all-done.4.parts = bf16[16,224,128]{2,1,0:T(8,128)(2,1)S(1)} async-done(((bf16[16,224,128]{2,1,0:T(8,128)(2,1)}), bf16[16,224,128]{2,1,0:T(8,128)(2,1)S(1)}, u32[]{:S(2)}, u32[]{:S(2)}) %all-to-all-start.4) | async-done | bytes 917536 | tf_op jit(solution)/shard_map/all_to_all | solution.py:452
  178.6 1.4 shard_map.97
  180.0 0.6 fusion.5
  (26 shorter events, 0.4 us)
Async XLA Ops:
  7.2 3.1 %copy-start.5 = (bf16[32]{0:T(256)(128)(2,1)S(1)}, bf16[32]{0:T(256)(128)(2,1)}, u32[]{:S(2)}) copy-start(bf16[32]{0:T(256)(128)(2,1)} %param.9) | copy-start | bytes 196
  7.2 49.3 %all-gather.4.cloned.1.call-start = ((), (), s32[]{:S(2)}) async-start(), calls=%async_computation.5 | async-start | bytes 7962624 | tf_op jit(solution)/shard_map/all_gather | solution.py:391
  7.9 7.9 %copy-start.4 = (s32[8,256]{1,0:T(8,128)S(1)}, s32[8,256]{1,0:T(8,128)}, u32[]{:S(2)}) copy-start(s32[8,256]{1,0:T(8,128)} %param.10) | copy-start | bytes 24580
  7.9 8.1 %copy-start.2 = (bf16[2,256,8,256]{3,2,1,0:T(8,128)(2,1)S(1)}, bf16[2,256,8,256]{3,2,1,0:T(8,128)(2,1)}, u32[]{:S(2)}) copy-start(bf16[2,256,8,256]{3,2,1,0:T(8,128)(2,1)} %param.6) | copy-start | bytes 6291460
  11.2 11.9 %all-to-all-start = ((bf16[8,33,384]{2,1,0:T(8,128)(2,1)}), bf16[8,33,384]{2,1,0:T(8,128)(2,1)S(1)}, u32[]{:S(2)}, u32[]{:S(2)}) async-start(bf16[8,33,384]{2,1,0:T(8,128)(2,1)} %pad_maximum_fusion), calls=%async_computation | async-start | bytes 491520 | tf_op jit(solution)/shard_map/all_to_all | solution.py:392
  15.7 113.2 %all-gather.6.cloned.1.call-start = ((), (), s32[]{:S(2)}) async-start(), calls=%async_computation.6 | async-start | bytes 6488064 | tf_op jit(solution)/shard_map/all_gather | solution.py:423
  23.3 34.2 %copy-start.3 = (bf16[1168,256]{1,0:T(8,128)(2,1)}, bf16[1168,256]{1,0:T(8,128)(2,1)S(1)}, u32[]{:S(2)}) copy-start(bf16[1168,256]{1,0:T(8,128)(2,1)S(1)} %fusion.1.middle) | copy-start | bytes 1794052
  23.3 17.0 %collective-permute-start.1 = (bf16[1168,256]{1,0:T(8,128)(2,1)S(1)}, bf16[1168,256]{1,0:T(8,128)(2,1)S(1)}, u32[]{:S(2)}, u32[]{:S(2)}) collective-permute-start(bf16[1168,256]{1,0:T(8,128)(2,1)S(1)} %fusion.1.middle), channel_id=1, source_target_pairs={{8,0},{16,8},{24,16},{32,24},{40,32},{48,40},{56,48},{64,56},{72,6... | collective-permute-start | bytes 1794056 | tf_op jit(solution)/shard_map/ppermute | solution.py:401
  24.6 16.9 %collective-permute-start = (bf16[1168,256]{1,0:T(8,128)(2,1)S(1)}, bf16[1168,256]{1,0:T(8,128)(2,1)S(1)}, u32[]{:S(2)}, u32[]{:S(2)}) collective-permute-start(bf16[1168,256]{1,0:T(8,128)(2,1)S(1)} %fusion.1.middle), channel_id=1, source_target_pairs={{0,8},{8,16},{16,24},{24,32},{32,40},{40,48},{48,56},{56,64},{64,7... | collective-permute-start | bytes 1794056 | tf_op jit(solution)/shard_map/ppermute | solution.py:400
  40.3 17.2 %copy-start.6 = (bf16[1168,256]{1,0:T(8,128)(2,1)}, bf16[1168,256]{1,0:T(8,128)(2,1)S(1)}, u32[]{:S(2)}) copy-start(bf16[1168,256]{1,0:T(8,128)(2,1)S(1)} %collective-permute-done.1.below) | copy-start | bytes 1794052
  41.5 16.0 %copy-start.7 = (bf16[1168,256]{1,0:T(8,128)(2,1)}, bf16[1168,256]{1,0:T(8,128)(2,1)S(1)}, u32[]{:S(2)}) copy-start(bf16[1168,256]{1,0:T(8,128)(2,1)S(1)} %collective-permute-done.above) | copy-start | bytes 1794052
  109.6 19.3 %all-to-all-start.2 = ((bf16[8,240,256]{2,1,0:T(8,128)(2,1)}), bf16[8,240,256]{2,1,0:T(8,128)(2,1)S(1)}, u32[]{:S(2)}, u32[]{:S(2)}) async-start(bf16[8,240,256]{2,1,0:T(8,128)(2,1)} %get-tuple-element.32), calls=%async_computation.2 | async-start | bytes 1966080 | tf_op jit(solution)/shard_map/all_to_all | solution.py:434
  128.9 2.6 %copy-start.1 = (bf16[11264,256]{1,0:T(8,128)(2,1)S(1)}, bf16[11264,256]{1,0:T(8,128)(2,1)}, u32[]{:S(2)}) copy-start(bf16[11264,256]{1,0:T(8,128)(2,1)} %all-gather.6.cloned.1.call-done) | copy-start | bytes 17301508
  135.8 0.9 copy-start
  136.8 22.9 %all-to-all-start.3 = ((bf16[16,224,128]{2,1,0:T(8,128)(2,1)}), bf16[16,224,128]{2,1,0:T(8,128)(2,1)S(1)}, u32[]{:S(2)}, u32[]{:S(2)}) async-start(bf16[16,224,128]{2,1,0:T(8,128)(2,1)} %copy-done), calls=%async_computation.3 | async-start | bytes 1835008 | tf_op jit(solution)/shard_map/all_to_all | solution.py:446
  160.8 17.8 %all-to-all-start.4 = ((bf16[16,224,128]{2,1,0:T(8,128)(2,1)}), bf16[16,224,128]{2,1,0:T(8,128)(2,1)S(1)}, u32[]{:S(2)}, u32[]{:S(2)}) async-start(bf16[16,224,128]{2,1,0:T(8,128)(2,1)} %shard_map.96), calls=%async_computation.4 | async-start | bytes 1835008 | tf_op jit(solution)/shard_map/all_to_all | solution.py:452
Sparse Core Ops, SparseCore 0:
  9.7 46.6 all-gather.3
  77.5 44.0 all-gather.5
